TPU v7x, 256 devices: a whole 4x4x8 slice. The times are simulated.
256 devices in a mesh: dp: 16 (over x_lo, z), fsdp: 16 (over x_hi, y, core).
Axes of the slice: x: 4 (x_hi: 2, x_lo: 2; x = x_hi * 2 + x_lo), y: 4, z: 8, core: 2. Of those that a mesh axis runs over, the one named last changes fastest.
Arguments:
- patches: bfloat16 [65536, 1792], P(('dp', 'fsdp')), may hold values from -12 to 12
- queries: bfloat16 [65536, 896], P(('dp', 'fsdp')), may hold values from -16 to 16
- keys: bfloat16 [65536, 896], P(('dp', 'fsdp')), may hold values from -16 to 16
- upstream: bfloat16 [65536, 1792], P(('dp', 'fsdp')), may hold values from -1 to 1
- value_weight: float32 [1792, 896], P('fsdp'), may hold values from -1 to 1
- output_weight: float32 [896, 1792], P('fsdp'), may hold values from -0.1875 to 0.1875
- value_first: float32 [1792, 896], P('fsdp'), may hold values from -6 to 6
- output_first: float32 [896, 1792], P('fsdp'), may hold values from -6 to 6
- value_second: float32 [1792, 896], P('fsdp'), may hold values from 1 to 50
- output_second: float32 [896, 1792], P('fsdp'), may hold values from 1 to 50
Outputs:
- value_weight_new: float32 [1792, 896], P('fsdp')
- output_weight_new: float32 [896, 1792], P('fsdp')
- value_first_new: float32 [1792, 896], P('fsdp')
- output_first_new: float32 [896, 1792], P('fsdp')
- value_second_new: float32 [1792, 896], P('fsdp')
- output_second_new: float32 [896, 1792], P('fsdp')
All inputs are finite; a program needn't handle non-finite values.
Results may differ from a plain program's by a relative error of at most 0.022.
Values may be sent and summed in bfloat16 or wider, within the bound.
A program may use at most 128 MiB of HBM per device.

v0:
```python
import jax
import jax.numpy as jnp
from jax import lax
from jax.sharding import PartitionSpec as P

HEADS = 8
HD = 112
SEQ = 256


learn_rate = 0.001
weight_decay = 0.1
beta_one = 0.9
beta_two = 0.999
adam_eps = 1e-08
first_fix = 0.9999734386011124
second_fix = 0.0952078528862911
rho_scale = 0.05


def norm_rows(rows):
    rows = rows.astype(jnp.float32)
    centred = rows - jnp.mean(rows, axis=-1, keepdims=True)
    return centred * lax.rsqrt(jnp.mean(centred * centred, axis=-1, keepdims=True) + 1e-06)


def attention_weights(queries, keys):
    query_heads = queries.reshape(-1, SEQ, HEADS, HD)
    key_heads = keys.reshape(-1, SEQ, HEADS, HD)
    scores = jnp.einsum(
        "bqhd,bkhd->bhqk", query_heads, key_heads, preferred_element_type=jnp.float32
    ) * HD ** (-0.5)
    scores = scores - jnp.max(scores, axis=-1, keepdims=True)
    expo = jnp.exp(scores)
    return (expo / jnp.sum(expo, axis=-1, keepdims=True)).astype(jnp.bfloat16)


def apply_heads(attention, values):
    rows = values.shape[0]
    heads = values.reshape(-1, SEQ, HEADS, HD)
    mixed = jnp.einsum("bhqk,bkhd->bqhd", attention, heads, preferred_element_type=jnp.float32)
    return mixed.reshape(rows, HEADS * HD).astype(jnp.bfloat16)


def apply_back(attention, d_mixed):
    rows = d_mixed.shape[0]
    heads = d_mixed.reshape(-1, SEQ, HEADS, HD)
    back = jnp.einsum("bhqk,bqhd->bkhd", attention, heads, preferred_element_type=jnp.float32)
    return back.reshape(rows, HEADS * HD).astype(jnp.bfloat16)


def contract_rows(left, right):
    return lax.dot_general(
        left, right, (((0,), (0,)), ((), ())), preferred_element_type=jnp.float32
    )


def local_grads(normed, patches, attention, upstream, values, output_b):
    mixed = apply_heads(attention, values)
    outcome = patches.astype(jnp.float32) + jnp.dot(
        mixed, output_b, preferred_element_type=jnp.float32
    )
    centred = outcome - jnp.mean(outcome, axis=-1, keepdims=True)
    inverse = lax.rsqrt(jnp.mean(centred * centred, axis=-1, keepdims=True) + 1e-06)
    normal_out = centred * inverse
    signal = upstream.astype(jnp.float32)
    d_outcome = inverse * (
        signal
        - jnp.mean(signal, axis=-1, keepdims=True)
        - normal_out * jnp.mean(signal * normal_out, axis=-1, keepdims=True)
    )
    d_outcome = d_outcome.astype(jnp.bfloat16)
    grad_output = contract_rows(mixed, d_outcome)
    d_mixed = lax.dot_general(
        d_outcome, output_b, (((1,), (1,)), ((), ())), preferred_element_type=jnp.float32
    ).astype(jnp.bfloat16)
    d_values = apply_back(attention, d_mixed)
    grad_value = contract_rows(normed, d_values)
    return (grad_value, grad_output)


def adam_update(weight, first, second, gradient):
    first_new = beta_one * first + (1.0 - beta_one) * gradient
    second_new = beta_two * second + (1.0 - beta_two) * gradient * gradient
    update = (
        first_new / first_fix / (jnp.sqrt(second_new / second_fix) + adam_eps)
        + weight_decay * weight
    )
    return (weight - learn_rate * update, first_new, second_new)


def on_device(
    patches,
    queries,
    keys,
    upstream,
    value_weight,
    output_weight,
    value_first,
    output_first,
    value_second,
    output_second,
):
    width = patches.shape[1]
    hidden = queries.shape[1]
    normed = norm_rows(patches).astype(jnp.bfloat16)
    attention = attention_weights(queries, keys)

    def gradients(value_owned, output_owned):
        value_full, output_full = (
            lax.all_gather(value_owned, "fsdp", axis=0, tiled=True),
            lax.all_gather(output_owned, "fsdp", axis=0, tiled=True),
        )
        values = jnp.dot(normed, value_full, preferred_element_type=jnp.float32).astype(
            jnp.bfloat16
        )
        return local_grads(normed, patches, attention, upstream, values, output_full)

    def combine(gradient_pair, want_norm):
        squares = None
        owned = (
            lax.psum_scatter(
                gradient_pair[0].astype(jnp.bfloat16), "fsdp", scatter_dimension=0, tiled=True
            ).astype(jnp.float32),
            lax.psum_scatter(
                gradient_pair[1].astype(jnp.bfloat16), "fsdp", scatter_dimension=0, tiled=True
            ).astype(jnp.float32),
        )
        owned = (
            lax.psum(owned[0].astype(jnp.bfloat16), "dp").astype(jnp.float32),
            lax.psum(owned[1].astype(jnp.bfloat16), "dp").astype(jnp.float32),
        )
        if want_norm:
            local_sq = jnp.sum(owned[0] * owned[0]) + jnp.sum(owned[1] * owned[1])
            squares = lax.psum(local_sq, "fsdp")
        return (owned, squares)

    first_pair, squares = combine(
        gradients(value_weight.astype(jnp.bfloat16), output_weight.astype(jnp.bfloat16)), True
    )
    mean_square = squares / (2.0 * width * hidden)
    stretch = rho_scale / jnp.sqrt(mean_square + 1e-06)
    shifted_value = (value_weight + stretch * first_pair[0]).astype(jnp.bfloat16)
    shifted_output = (output_weight + stretch * first_pair[1]).astype(jnp.bfloat16)
    second_pair, unused_norm = combine(gradients(shifted_value, shifted_output), False)
    value_new, value_first_new, value_second_new = adam_update(
        value_weight, value_first, value_second, second_pair[0]
    )
    output_new, output_first_new, output_second_new = adam_update(
        output_weight, output_first, output_second, second_pair[1]
    )
    return (
        value_new,
        output_new,
        value_first_new,
        output_first_new,
        value_second_new,
        output_second_new,
    )


def solution(mesh):
    return jax.shard_map(
        on_device,
        mesh=mesh,
        in_specs=(
            P(("dp", "fsdp"), None),
            P(("dp", "fsdp"), None),
            P(("dp", "fsdp"), None),
            P(("dp", "fsdp"), None),
            P("fsdp", None),
            P("fsdp", None),
            P("fsdp", None),
            P("fsdp", None),
            P("fsdp", None),
            P("fsdp", None),
        ),
        out_specs=(
            P("fsdp", None),
            P("fsdp", None),
            P("fsdp", None),
            P("fsdp", None),
            P("fsdp", None),
            P("fsdp", None),
        ),
        check_vma=False,
    )
```

profile of v0, /device:TPU:8, one launch (start us, length us, event | category | flops | bytes accessed | tf_op | source)
XLA Modules:
  0.0 916.1 jit_solution(1716903948482862718)
XLA Ops:
  7.2 1.8 convert_element_type.128
  9.1 1.7 convert_element_type.135
  10.9 0.2 copy.27
  11.1 0.2 copy.28
  11.6 0.4 fusion.10
  12.0 2.2 fusion.40
  14.2 1.8 divide_convert_fusion
  16.0 53.9 %all-gather.5.cloned.1.call-done = bf16[1792,896]{1,0:T(8,128)(2,1)} async-done(((bf16[112,896]{1,0:T(8,128)(2,1)}), bf16[1792,896]{1,0:T(8,128)(2,1)}) %all-gather.5.cloned.1.call-update) | async-done | bytes 3211280 | tf_op jit(solution)/shard_map/all_gather | solution.py:111
  69.9 3.1 convolution_convert_fusion.7
  73.0 0.2 copy.26
  73.2 0.3 convolution_convert_fusion.11
  73.5 54.5 %all-gather.7.cloned.1.call-done = bf16[896,1792]{1,0:T(8,128)(2,1)} async-done(((bf16[56,1792]{1,0:T(8,128)(2,1)}), bf16[896,1792]{1,0:T(8,128)(2,1)}) %all-gather.7.cloned.1.call-update) | async-done | bytes 3211280 | tf_op jit(solution)/shard_map/all_gather | solution.py:112
  128.0 3.1 fusion.41
  131.1 0.3 multiply_reduce_fusion.2
  131.5 0.8 copy-done.3
  132.3 0.6 convert_reduce_fusion
  132.9 2.9 convolution_convert_fusion.2
  135.9 3.4 convolution_convert_fusion.6
  139.3 0.2 copy.30
  139.5 1.7 convolution_convert_fusion.10
  141.2 3.0 convolution_convert_fusion.3
  144.3 75.3 %reduce-scatter.7.cloned.1.call-done = bf16[56,1792]{1,0:T(8,128)(2,1)} async-done(((bf16[896,1792]{1,0:T(8,128)(2,1)}), bf16[56,1792]{1,0:T(8,128)(2,1)}) %reduce-scatter.7.cloned.1.call-update) | async-done | bytes 200720 | tf_op jit(solution)/shard_map/reduce_scatter | solution.py:125
  219.6 87.6 %reduce-scatter.5.cloned.1.call-done = bf16[112,896]{1,0:T(8,128)(2,1)} async-done(((bf16[1792,896]{1,0:T(8,128)(2,1)}), bf16[112,896]{1,0:T(8,128)(2,1)}) %reduce-scatter.5.cloned.1.call-update) | async-done | bytes 200720 | tf_op jit(solution)/shard_map/reduce_scatter | solution.py:122
  307.2 134.2 %all-reduce.7.cloned.1.call-done = (bf16[56,1792]{1,0:T(8,128)(2,1)}, bf16[112,896]{1,0:T(8,128)(2,1)}) async-done(((bf16[56,1792]{1,0:T(8,128)(2,1)}, bf16[112,896]{1,0:T(8,128)(2,1)}), (bf16[56,1792]{1,0:T(8,128)(2,1)}, bf16[112,896]{1,0:T(8,128)(2,1)})) %all-reduce.7.cloned.1.call-update) | async-done | bytes 401424 | tf_op jit(solution)/shard_map/psum | solution.py:131
  441.4 1.6 fusion.15
  443.1 1.6 fusion.18
  446.0 28.3 %psum.37 = f32[]{:T(128)} all-reduce(f32[]{:T(128)S(6)} %add.93), channel_id=1, replica_groups=mesh['dp'=16,'fsdp'=16] {'fsdp'}, use_global_device_ids=true, to_apply=%region_14.0 | all-reduce | flops 1 | bytes 8 | tf_op jit(solution)/shard_map/psum | solution.py:135
  475.0 1.7 fusion.17
  476.7 1.7 fusion.20
  478.4 0.2 reduce-scatter.11.cloned.1.call-start
  478.7 54.4 %all-gather.9.cloned.1.call-done = bf16[1792,896]{1,0:T(8,128)(2,1)} async-done(((bf16[112,896]{1,0:T(8,128)(2,1)}), bf16[1792,896]{1,0:T(8,128)(2,1)}) %all-gather.9.cloned.1.call-update) | async-done | bytes 3211280 | tf_op jit(solution)/shard_map/all_gather | solution.py:111
  533.1 3.1 convolution_convert_fusion.5
  536.2 0.2 copy.32
  536.4 0.3 convolution_convert_fusion.9
  536.7 54.9 %all-gather.11.cloned.1.call-done = bf16[896,1792]{1,0:T(8,128)(2,1)} async-done(((bf16[56,1792]{1,0:T(8,128)(2,1)}), bf16[896,1792]{1,0:T(8,128)(2,1)}) %all-gather.11.cloned.1.call-update) | async-done | bytes 3211280 | tf_op jit(solution)/shard_map/all_gather | solution.py:112
  591.6 3.1 fusion.42
  594.7 0.3 multiply_reduce_fusion.1
  595.1 0.8 copy-done.4
  595.9 0.5 fusion.13
  596.4 2.9 convolution_convert_fusion
  599.4 3.4 convolution_convert_fusion.4
  603.0 1.7 convolution_convert_fusion.8
  604.7 3.0 convolution_convert_fusion.1
  607.8 75.2 %reduce-scatter.11.cloned.1.call-done = bf16[56,1792]{1,0:T(8,128)(2,1)} async-done(((bf16[896,1792]{1,0:T(8,128)(2,1)}), bf16[56,1792]{1,0:T(8,128)(2,1)}) %reduce-scatter.11.cloned.1.call-update) | async-done | bytes 200720 | tf_op jit(solution)/shard_map/reduce_scatter | solution.py:125
  683.0 88.4 %reduce-scatter.9.cloned.1.call-done = bf16[112,896]{1,0:T(8,128)(2,1)} async-done(((bf16[1792,896]{1,0:T(8,128)(2,1)}), bf16[112,896]{1,0:T(8,128)(2,1)}) %reduce-scatter.9.cloned.1.call-update) | async-done | bytes 200720 | tf_op jit(solution)/shard_map/reduce_scatter | solution.py:122
  771.5 134.4 %all-reduce.5.cloned.1.call-done = (bf16[112,896]{1,0:T(8,128)(2,1)}, bf16[56,1792]{1,0:T(8,128)(2,1)}) async-done(((bf16[112,896]{1,0:T(8,128)(2,1)}, bf16[56,1792]{1,0:T(8,128)(2,1)}), (bf16[112,896]{1,0:T(8,128)(2,1)}, bf16[56,1792]{1,0:T(8,128)(2,1)})) %all-reduce.5.cloned.1.call-update) | async-done | bytes 401424 | tf_op jit(solution)/shard_map/psum | solution.py:130
  905.9 2.2 multiply_subtract_fusion.1
  908.1 1.2 multiply_subtract_fusion
  (59 shorter events, 1.1 us)
Async XLA Ops:
  7.2 3.8 copy-start.9
  7.2 4.0 copy-start.10
  7.2 4.2 copy-start
  7.2 62.7 %all-gather.5.cloned.1.call-start = ((), (), s32[]{:S(2)}) async-start(), calls=%async_computation.4 | async-start | bytes 3411968 | tf_op jit(solution)/shard_map/all_gather | solution.py:111
  9.1 118.9 %all-gather.7.cloned.1.call-start = ((), (), s32[]{:S(2)}) async-start(), calls=%async_computation.5 | async-start | bytes 3411968 | tf_op jit(solution)/shard_map/all_gather | solution.py:112
  10.9 208.7 %reduce-scatter.7.cloned.1.call-start = ((), (), s32[]{:S(2)}) async-start(), calls=%async_computation.7 | async-start | bytes 3411968 | tf_op jit(solution)/shard_map/reduce_scatter | solution.py:125
  16.0 57.2 %copy-start.1 = (bf16[8,256,256]{1,2,0:T(8,128)(2,1)}, bf16[8,256,256]{1,2,0:T(8,128)(2,1)S(1)}, u32[]{:S(2)}) copy-start(bf16[8,256,256]{1,2,0:T(8,128)(2,1)S(1)} %divide_convert_fusion) | copy-start | bytes 3145732
  131.1 1.2 copy-start.3
  135.8 171.3 %reduce-scatter.5.cloned.1.call-start = ((), (), s32[]{:S(2)}) async-start(), calls=%async_computation.6 | async-start | bytes 3411968 | tf_op jit(solution)/shard_map/reduce_scatter | solution.py:122
  144.2 330.8 %copy-start.5 = (f32[112,896]{1,0:T(8,128)S(1)}, f32[112,896]{1,0:T(8,128)}, u32[]{:S(2)}) copy-start(f32[112,896]{1,0:T(8,128)} %param.14) | copy-start | bytes 1204228
  144.2 332.5 %copy-start.7 = (f32[56,1792]{1,0:T(8,128)S(1)}, f32[56,1792]{1,0:T(8,128)}, u32[]{:S(2)}) copy-start(f32[56,1792]{1,0:T(8,128)} %param.15) | copy-start | bytes 1204228
  144.2 297.2 %all-reduce.7.cloned.1.call-start = ((), (), s32[]{:S(2)}) async-start(), calls=%async_computation.13 | async-start | bytes 802816 | tf_op jit(solution)/shard_map/psum | solution.py:131
  307.1 226.0 %all-gather.9.cloned.1.call-start = ((), (), s32[]{:S(2)}) async-start(), calls=%async_computation.8 | async-start | bytes 3411968 | tf_op jit(solution)/shard_map/all_gather | solution.py:111
  476.7 114.9 %all-gather.11.cloned.1.call-start = ((), (), s32[]{:S(2)}) async-start(), calls=%async_computation.9 | async-start | bytes 3411968 | tf_op jit(solution)/shard_map/all_gather | solution.py:112
  478.4 58.0 %copy-start.2 = (bf16[8,256,256]{1,2,0:T(8,128)(2,1)S(1)}, bf16[8,256,256]{1,2,0:T(8,128)(2,1)}, u32[]{:S(2)}) copy-start(bf16[8,256,256]{1,2,0:T(8,128)(2,1)} %copy-done.1) | copy-start | bytes 3145732
  478.4 204.6 %reduce-scatter.11.cloned.1.call-start = ((), (), s32[]{:S(2)}) async-start(), calls=%async_computation.11 | async-start | bytes 3411968 | tf_op jit(solution)/shard_map/reduce_scatter | solution.py:125
  594.7 1.2 copy-start.4
  599.3 172.1 %reduce-scatter.9.cloned.1.call-start = ((), (), s32[]{:S(2)}) async-start(), calls=%async_computation.10 | async-start | bytes 3411968 | tf_op jit(solution)/shard_map/reduce_scatter | solution.py:122
  607.7 298.2 %copy-start.6 = (f32[112,896]{1,0:T(8,128)S(1)}, f32[112,896]{1,0:T(8,128)}, u32[]{:S(2)}) copy-start(f32[112,896]{1,0:T(8,128)} %param.14) | copy-start | bytes 1204228
  607.7 298.2 %copy-start.11 = (f32[112,896]{1,0:T(8,128)S(1)}, f32[112,896]{1,0:T(8,128)}, u32[]{:S(2)}) copy-start(f32[112,896]{1,0:T(8,128)} %param.16) | copy-start | bytes 1204228
  607.7 298.2 %copy-start.12 = (f32[112,896]{1,0:T(8,128)S(1)}, f32[112,896]{1,0:T(8,128)}, u32[]{:S(2)}) copy-start(f32[112,896]{1,0:T(8,128)} %param.18) | copy-start | bytes 1204228
  607.7 300.4 %copy-start.8 = (f32[56,1792]{1,0:T(8,128)S(1)}, f32[56,1792]{1,0:T(8,128)}, u32[]{:S(2)}) copy-start(f32[56,1792]{1,0:T(8,128)} %param.15) | copy-start | bytes 1204228
  607.7 300.4 %copy-start.13 = (f32[56,1792]{1,0:T(8,128)S(1)}, f32[56,1792]{1,0:T(8,128)}, u32[]{:S(2)}) copy-start(f32[56,1792]{1,0:T(8,128)} %param.17) | copy-start | bytes 1204228
  607.7 300.3 %copy-start.14 = (f32[56,1792]{1,0:T(8,128)S(1)}, f32[56,1792]{1,0:T(8,128)}, u32[]{:S(2)}) copy-start(f32[56,1792]{1,0:T(8,128)} %param.19) | copy-start | bytes 1204228
  607.7 298.1 %all-reduce.5.cloned.1.call-start = ((), (), s32[]{:S(2)}) async-start(), calls=%async_computation.12 | async-start | bytes 802816 | tf_op jit(solution)/shard_map/psum | solution.py:130
  905.9 2.2 copy-start.15
Sparse Core Ops, SparseCore 0:
  11.3 58.5 all-gather.4
  73.1 54.8 all-gather.6
  136.0 83.5 reduce-scatter.6
  223.8 83.3 reduce-scatter.4
  309.7 131.7 all-reduce.6
  476.8 56.2 all-gather.8
  536.7 54.8 all-gather.10
  599.4 83.5 reduce-scatter.10
  688.0 83.3 reduce-scatter.8
  774.2 131.6 all-reduce.4
where the time goes:
time: 917 us; the launch traced here: 916 us
  waiting for transfers between devices  813 us (89%)
  matrix products  37.2 us (4%)
  blocking collectives  28.3 us (3%)
  other arithmetic  17.6 us (2%)
  between operations  16.4 us (2%)
    reduce_scatter x2, waiting for transfers between devices, combine(): lax.psum_scatter(gradient_pair[0].astype(jnp.bfloat16), 'fsdp', scatter_d...  176 us
    reduce_scatter x2, waiting for transfers between devices, combine(): lax.psum_scatter(gradient_pair[1].astype(jnp.bfloat16), 'fsdp', scatter_d...  151 us
    psum x1, waiting for transfers between devices, combine(): lax.psum(owned[0].astype(jnp.bfloat16), 'dp').astype(jnp.float32)  134 us
    psum x1, waiting for transfers between devices, combine(): lax.psum(owned[1].astype(jnp.bfloat16), 'dp').astype(jnp.float32)  134 us
    all_gather x2, waiting for transfers between devices, gradients(): lax.all_gather(output_owned, 'fsdp', axis=0, tiled=True)  109 us
    all_gather x2, waiting for transfers between devices, gradients(): lax.all_gather(value_owned, 'fsdp', axis=0, tiled=True)  108 us
    psum x1, blocking collectives, combine(): squares = lax.psum(local_sq, 'fsdp')  28.3 us
  transfers between devices with their start and end apart: 10, of which 10 were waited for; matrix products, arithmetic and copies ran while one was open for 4% of the time, Pallas kernels for 0%

commit v1 on v0

v1 whole, which is shorter than its diff:
```python
import functools

import jax
import jax.numpy as jnp
from jax import lax
from jax.experimental import pallas as pl
from jax.experimental.pallas import tpu as pltpu
from jax.sharding import PartitionSpec as P

HEADS = 8
HD = 112
SEQ = 256
D = 1792
HID = 896
BLOCKS = 7
WIDTHS = (512, 384)
MESH = pl.DeviceIdType.MESH
BF = jnp.bfloat16
F32 = jnp.float32


learn_rate = 0.001
weight_decay = 0.1
beta_one = 0.9
beta_two = 0.999
adam_eps = 1e-08
first_fix = 0.9999734386011124
second_fix = 0.0952078528862911
rho_scale = 0.05


def place():
    dp = lax.axis_index("dp")
    fs = lax.axis_index("fsdp")
    return (fs // 8) * 2 + dp // 8, (fs // 2) % 4, dp % 8, fs % 2


def device(x, y, z, c):
    return ((x % 2) * 8 + z, (x // 2) * 8 + y * 2 + c)


def slot(x):
    return (x % 2) * 2 + x // 2


class Net:
    def __init__(self):
        self.x, self.y, self.z, self.c = place()

    def core(self):
        return device(self.x, self.y, self.z, 1 - self.c)

    def along(self, axis, step):
        if axis == "x":
            return device((self.x + step) % 4, self.y, self.z, self.c)
        if axis == "y":
            return device(self.x, (self.y + step) % 4, self.z, self.c)
        return device(self.x, self.y, (self.z + step) % 8, self.c)

    def spot(self, axis, step=0):
        if axis == "x":
            return slot((self.x + step) % 4)
        if axis == "y":
            return (self.y + step) % 4
        return (self.z + step) % 8

    def barrier(self):
        sem = pltpu.get_barrier_semaphore()
        targets = [self.core()]
        targets += [self.along("x", s) for s in (1, 2, 3)]
        targets += [self.along("y", s) for s in (1, 2, 3)]
        targets += [self.along("z", s) for s in range(1, 8)]
        for t in targets:
            pl.semaphore_signal(sem, inc=1, device_id=t, device_id_type=MESH)
        pl.semaphore_wait(sem, len(targets))


def push(src, dst, send, recv, target):
    copy = pltpu.make_async_remote_copy(
        src_ref=src, dst_ref=dst, send_sem=send, recv_sem=recv, device_id=target, device_id_type=MESH
    )
    copy.start()
    return copy


def add_blocks(count, write, *reads):
    def step(i, carry):
        total = reads[0](i).astype(F32)
        for read in reads[1:]:
            total = total + read(i).astype(F32)
        write(i, total.astype(BF))
        return carry

    lax.fori_loop(0, count, step, 0)


def ordered(part):
    return ("x", "y") if part == 0 else ("y", "x")


def grid_at(ref, part, first, second):
    return ref.at[first, second] if part == 0 else ref.at[second, first]


def reduce_scratch():
    shapes = []
    for w in WIDTHS:
        shapes += [
            pltpu.VMEM((4, 4, BLOCKS, 16, w), BF),
            pltpu.VMEM((4, 4, BLOCKS, 16, w), BF),
            pltpu.VMEM((2, 2, BLOCKS, 16, w), BF),
            pltpu.VMEM((2, 4, BLOCKS, 16, w), BF),
            pltpu.VMEM((4, BLOCKS, 16, w), BF),
            pltpu.VMEM((3, BLOCKS, 16, w), BF),
            pltpu.VMEM((BLOCKS, 16, w), BF),
            pltpu.VMEM((7, 16, w), BF),
            pltpu.SemaphoreType.DMA((2, 4 + 2 + 4 + 3 + 7)),
        ]
    return shapes


def reduce_all(net, grads, outs, scratch):
    state = []
    for part in (0, 1):
        state.append(scratch[part * 9:part * 9 + 9])
    rows = []
    cores = [[], []]
    for step in (2, 1, 3, 0):
        for part in (0, 1):
            other, sums, far, mine, _, _, _, _, sem = state[part]
            first = ordered(part)[0]
            i = net.spot(first, step)
            j = len(cores[part])
            if part == 0:
                src, dst = grads[part].at[i, :, 1 - net.c], other.at[i]
            else:
                src, dst = grads[part].at[:, i, 1 - net.c], other.at[:, i]
            cores[part].append(push(src, dst, sem.at[0, j], sem.at[1, j], net.core()))
    waits = []

    def half_of(ref, part, i, h):
        return ref.at[i, pl.ds(2 * h, 2)] if part == 0 else ref.at[pl.ds(2 * h, 2), i]

    near = [[None] * 6, [None] * 6]
    for j, step in enumerate((2, 1, 3, 0)):
        for part in (0, 1):
            other, sums, far, mine, _, _, _, _, sem = state[part]
            first = ordered(part)[0]
            i = net.spot(first, step)
            cores[part][j].wait_recv()
            g = grads[part]
            if part == 0:
                def write(k, v):
                    sums[i, k] = v
                add_blocks(4, write, lambda k: g[i, k, net.c], lambda k: other[i, k])
            else:
                def write(k, v):
                    sums[k, i] = v
                add_blocks(4, write, lambda k: g[k, i, net.c], lambda k: other[k, i])
            right, left = net.along(first, 1), net.along(first, 3)
            if step == 2:
                near[part][0] = push(half_of(sums, part, i, 0), far.at[0], sem.at[0, 4], sem.at[1, 4], right)
                near[part][1] = push(half_of(sums, part, i, 1), far.at[1], sem.at[0, 5], sem.at[1, 5], left)
            if step == 1:
                near[part][2] = push(half_of(sums, part, i, 1), mine.at[0, pl.ds(2, 2)], sem.at[0, 6], sem.at[1, 6], right)
            if step == 3:
                near[part][3] = push(half_of(sums, part, i, 0), mine.at[1, pl.ds(0, 2)], sem.at[0, 7], sem.at[1, 7], left)
    for part in (0, 1):
        other, sums, far, mine, _, _, _, _, sem = state[part]
        first = ordered(part)[0]
        right, left = net.along(first, 1), net.along(first, 3)
        r, l = net.spot(first, 1), net.spot(first, 3)
        near[part][0].wait_recv()
        if part == 0:
            def write(k, v):
                sums[r, k] = v
            add_blocks(2, write, lambda k: sums[r, k], lambda k: far[0, k])
        else:
            def write(k, v):
                sums[k, r] = v
            add_blocks(2, write, lambda k: sums[k, r], lambda k: far[0, k])
        near[part][4] = push(half_of(sums, part, r, 0), mine.at[0, pl.ds(0, 2)], sem.at[0, 8], sem.at[1, 8], right)
        near[part][1].wait_recv()
        if part == 0:
            def write(k, v):
                sums[l, k + 2] = v
            add_blocks(2, write, lambda k: sums[l, k + 2], lambda k: far[1, k])
        else:
            def write(k, v):
                sums[k + 2, l] = v
            add_blocks(2, write, lambda k: sums[k + 2, l], lambda k: far[1, k])
        near[part][5] = push(half_of(sums, part, l, 1), mine.at[1, pl.ds(2, 2)], sem.at[0, 9], sem.at[1, 9], left)
    second_copies = [[], []]
    for part in (0, 1):
        other, sums, far, mine, row, from_row, _, _, sem = state[part]
        first, second = ordered(part)
        me = net.spot(first)
        for k in (2, 3, 4, 5):
            near[part][k].wait_recv()

        def write(k, v):
            row[k] = v
        if part == 0:
            add_blocks(4, write, lambda k: sums[me, k], lambda k: mine[0, k], lambda k: mine[1, k])
        else:
            add_blocks(4, write, lambda k: sums[k, me], lambda k: mine[0, k], lambda k: mine[1, k])
        for d in (2, 1, 3):
            second_copies[part].append(
                push(row.at[net.spot(second, d)], from_row.at[d - 1], sem.at[0, 9 + d], sem.at[1, 9 + d], net.along(second, d))
            )
    for part in (0, 1):
        other, sums, far, mine, row, from_row, line, from_line, sem = state[part]
        second = ordered(part)[1]
        me = net.spot(second)
        for copy in second_copies[part]:
            copy.wait_recv()

        def write(k, v):
            line[k] = v
        add_blocks(BLOCKS, write, lambda k: row[me, k], lambda k: from_row[0, k], lambda k: from_row[1, k], lambda k: from_row[2, k])
        for d in (4, 3, 5, 2, 6, 1, 7):
            z = net.spot("z", d)

            @pl.when(z != 7)
            def _():
                push(line.at[z], from_line.at[d - 1], sem.at[0, 12 + d], sem.at[1, 12 + d], net.along("z", d))
    for part in (0, 1):
        other, sums, far, mine, row, from_row, line, from_line, sem = state[part]

        @pl.when(net.z != 7)
        def _():
            for d in range(1, 8):
                pltpu.make_async_remote_copy(
                    src_ref=line.at[0], dst_ref=from_line.at[d - 1], send_sem=sem.at[0, 12 + d], recv_sem=sem.at[1, 12 + d],
                    device_id=net.along("z", d), device_id_type=MESH,
                ).wait_recv()
            total = line[net.z].astype(F32)
            for d in range(7):
                total = total + from_line[d].astype(F32)
            outs[part][...] = total.astype(BF)

    def drain():
        for part in (0, 1):
            other, sums, far, mine, row, from_row, line, from_line, sem = state[part]
            for copy in cores[part] + near[part] + second_copies[part]:
                copy.wait_send()
            for d in range(1, 8):
                @pl.when(net.spot("z", d) != 7)
                def _():
                    pltpu.make_async_remote_copy(
                        src_ref=line.at[0], dst_ref=from_line.at[d - 1], send_sem=sem.at[0, 12 + d], recv_sem=sem.at[1, 12 + d],
                        device_id=net.along("z", d), device_id_type=MESH,
                    ).wait_send()
    return drain


def gather_scratch():
    return [pltpu.SemaphoreType.DMA((2, 3 + 6 + 8)) for _ in WIDTHS]


def gather_all(net, fulls, sems):
    seconds = [[], []]
    for part in (0, 1):
        second = ordered(part)[1]
        own = fulls[part].at[net.spot("x"), net.spot("y"), net.c]
        for d in (2, 1, 3):
            seconds[part].append(push(own, own, sems[part].at[0, d - 1], sems[part].at[1, d - 1], net.along(second, d)))

    def line(part, i, h):
        ref = fulls[part]
        return ref.at[i, pl.ds(2 * h, 2), net.c] if part == 0 else ref.at[pl.ds(2 * h, 2), i, net.c]

    def whole(part, i):
        ref = fulls[part]
        return ref.at[i, :, net.c] if part == 0 else ref.at[:, i, net.c]

    copies = [[], []]
    cores = [[], []]
    for part in (0, 1):
        first = ordered(part)[0]
        for copy in seconds[part]:
            copy.wait_recv()
        right, left = net.along(first, 1), net.along(first, 3)
        me = net.spot(first)
        sem = sems[part]
        for j, (h, to) in enumerate(((0, right), (1, left), (1, right), (0, left))):
            copies[part].append(push(line(part, me, h), line(part, me, h), sem.at[0, 3 + j], sem.at[1, 3 + j], to))
        cores[part].append(push(whole(part, me), whole(part, me), sem.at[0, 9], sem.at[1, 9], net.core()))
    for part in (0, 1):
        first = ordered(part)[0]
        right, left = net.along(first, 1), net.along(first, 3)
        r, l = net.spot(first, 1), net.spot(first, 3)
        sem = sems[part]
        copies[part][0].wait_recv()
        copies[part].append(push(line(part, l, 0), line(part, l, 0), sem.at[0, 7], sem.at[1, 7], right))
        copies[part][1].wait_recv()
        copies[part].append(push(line(part, r, 1), line(part, r, 1), sem.at[0, 8], sem.at[1, 8], left))
        cores[part].append(push(line(part, l, 0), line(part, l, 0), sem.at[0, 10], sem.at[1, 10], net.core()))
        cores[part].append(push(line(part, r, 1), line(part, r, 1), sem.at[0, 11], sem.at[1, 11], net.core()))
    for part in (0, 1):
        first = ordered(part)[0]
        r, l, far = net.spot(first, 1), net.spot(first, 3), net.spot(first, 2)
        sem = sems[part]
        for k, i, h in ((2, l, 1), (3, r, 0), (4, far, 0), (5, far, 1)):
            copies[part][k].wait_recv()
            cores[part].append(push(line(part, i, h), line(part, i, h), sem.at[0, 10 + k], sem.at[1, 10 + k], net.core()))
    for part in (0, 1):
        for copy in cores[part]:
            copy.wait_recv()
        for copy in seconds[part] + copies[part] + cores[part]:
            copy.wait_send()


def weights_kernel(own_a, own_b, full_a, full_b, sem_a, sem_b, copy_sem):
    net = Net()
    net.barrier()
    fulls = (full_a, full_b)
    for part, own in enumerate((own_a, own_b)):
        copy = pltpu.make_async_copy(own.at[net.x % 2], fulls[part].at[net.spot("x"), net.spot("y"), net.c], copy_sem.at[part])
        copy.start()
        copy.wait()
    gather_all(net, fulls, (sem_a, sem_b))


def spread_line(net, fulls, outs, sems):
    for part in (0, 1):
        @pl.when(net.z != 7)
        def _():
            dst = fulls[part].at[net.spot("x"), net.spot("y"), net.c, net.z]
            dst[...] = outs[part][...]
            for d in (4, 3, 5, 2, 6, 1, 7):
                push(dst, dst, sems[part].at[0, d - 1], sems[part].at[1, d - 1], net.along("z", d))


def wait_line(net, fulls, sems, recv):
    for part in (0, 1):
        for d in range(1, 8):
            z = net.z if not recv else (net.z + 8 - d) % 8
            block = fulls[part].at[net.spot("x"), net.spot("y"), net.c, jnp.minimum(z, 6)]

            @pl.when(z != 7)
            def _():
                copy = pltpu.make_async_remote_copy(
                    src_ref=block, dst_ref=block, send_sem=sems[part].at[0, d - 1], recv_sem=sems[part].at[1, d - 1],
                    device_id=net.along("z", d), device_id_type=MESH,
                )
                if recv:
                    copy.wait_recv()
                else:
                    copy.wait_send()


def middle_kernel(grad_a, grad_b, full_a, full_b, out_a, out_b, line_a, line_b, sem_a, sem_b, *scratch):
    net = Net()
    net.barrier()
    fulls, outs = (full_a, full_b), (out_a, out_b)
    drain = reduce_all(net, (grad_a, grad_b), outs, scratch)
    spread_line(net, fulls, outs, (line_a, line_b))
    wait_line(net, fulls, (line_a, line_b), True)
    gather_all(net, fulls, (sem_a, sem_b))
    wait_line(net, fulls, (line_a, line_b), False)
    drain()


def last_kernel(grad_a, grad_b, owned_a, owned_b, out_a, out_b, line_a, line_b, pair_a, pair_b, *scratch):
    net = Net()
    net.barrier()
    owned, outs = (owned_a, owned_b), (out_a, out_b)
    drain = reduce_all(net, (grad_a, grad_b), outs, scratch)
    half = net.x % 2
    partner = device(net.x + 1 - 2 * half, net.y, net.z, net.c)

    def block(part, z):
        return owned[part].at[half, jnp.minimum(z, 6)]

    def line_copy(part, d, z):
        sems = (line_a, line_b)[part]
        return pltpu.make_async_remote_copy(
            src_ref=block(part, z), dst_ref=block(part, z), send_sem=sems.at[0, d - 1], recv_sem=sems.at[1, d - 1],
            device_id=net.along("z", d), device_id_type=MESH,
        )

    def pair_copy(part, d, z):
        sems = (pair_a, pair_b)[part]
        return pltpu.make_async_remote_copy(
            src_ref=block(part, z), dst_ref=block(part, z), send_sem=sems.at[0, d], recv_sem=sems.at[1, d],
            device_id=partner, device_id_type=MESH,
        )

    for part in (0, 1):
        @pl.when(net.z != 7)
        def _():
            owned[part][half, net.z] = outs[part][...]
            for d in (4, 3, 5, 2, 6, 1, 7):
                line_copy(part, d, net.z).start()
            pair_copy(part, 0, net.z).start()
    for d in (1, 7, 2, 6, 3, 5, 4):
        z = (net.z + 8 - d) % 8

        @pl.when(z != 7)
        def _():
            for part in (0, 1):
                line_copy(part, d, z).wait_recv()
                pair_copy(part, d, z).start()
    for d in range(8):
        z = (net.z + 8 - d) % 8

        @pl.when(z != 7)
        def _():
            for part in (0, 1):
                pair_copy(part, d, z).wait()
    for part in (0, 1):
        @pl.when(net.z != 7)
        def _():
            for d in range(1, 8):
                line_copy(part, d, net.z).wait_send()
    drain()


def vmem(n):
    return [pl.BlockSpec(memory_space=pltpu.VMEM)] * n


def params(cid):
    return pltpu.CompilerParams(collective_id=cid, has_side_effects=True, vmem_limit_bytes=60 * 2**20)


def full_shapes():
    return tuple(jax.ShapeDtypeStruct((4, 4, 2, BLOCKS, 16, w), BF) for w in WIDTHS)


def gather_weights(own):
    a, b = own[..., :WIDTHS[0]], own[..., WIDTHS[0]:]
    return pl.pallas_call(
        weights_kernel,
        out_shape=full_shapes(),
        in_specs=vmem(2),
        out_specs=vmem(2),
        scratch_shapes=gather_scratch() + [pltpu.SemaphoreType.DMA((2,))],
        name="gather_weights",
        compiler_params=params(0),
    )(a, b)


def line_sems(n=7):
    return [pltpu.SemaphoreType.DMA((2, n)) for _ in WIDTHS]


def block_scratch():
    return [pltpu.VMEM((16, w), BF) for w in WIDTHS]


def sum_and_gather(grads):
    return pl.pallas_call(
        middle_kernel,
        out_shape=full_shapes(),
        in_specs=vmem(2),
        out_specs=vmem(2),
        scratch_shapes=block_scratch() + line_sems() + gather_scratch() + reduce_scratch(),
        name="sum_and_gather",
        compiler_params=params(1),
    )(*grads)


def sum_owned(grads):
    return pl.pallas_call(
        last_kernel,
        out_shape=tuple(jax.ShapeDtypeStruct((2, BLOCKS, 16, w), BF) for w in WIDTHS),
        in_specs=vmem(2),
        out_specs=vmem(2),
        scratch_shapes=block_scratch() + line_sems() + line_sems(8) + reduce_scratch(),
        name="sum_owned",
        compiler_params=params(2),
    )(*grads)


def norm_rows(rows):
    rows = rows.astype(F32)
    centred = rows - jnp.mean(rows, axis=-1, keepdims=True)
    return centred * lax.rsqrt(jnp.mean(centred * centred, axis=-1, keepdims=True) + 1e-06)


def attention_weights(queries, keys):
    query_heads = queries.reshape(-1, SEQ, HEADS, HD)
    key_heads = keys.reshape(-1, SEQ, HEADS, HD)
    scores = jnp.einsum("bqhd,bkhd->bhqk", query_heads, key_heads, preferred_element_type=F32) * HD ** (-0.5)
    scores = scores - jnp.max(scores, axis=-1, keepdims=True)
    expo = jnp.exp(scores)
    return (expo / jnp.sum(expo, axis=-1, keepdims=True)).astype(BF)


def apply_heads(attention, values):
    rows = values.shape[0]
    heads = values.reshape(-1, SEQ, HEADS, HD)
    mixed = jnp.einsum("bhqk,bkhd->bqhd", attention, heads, preferred_element_type=F32)
    return mixed.reshape(rows, HEADS * HD).astype(BF)


def apply_back(attention, d_mixed):
    rows = d_mixed.shape[0]
    heads = d_mixed.reshape(-1, SEQ, HEADS, HD)
    back = jnp.einsum("bhqk,bqhd->bkhd", attention, heads, preferred_element_type=F32)
    return back.reshape(rows, HEADS * HD).astype(BF)


def contract_rows(left, right):
    return lax.dot_general(left, right, (((0,), (0,)), ((), ())), preferred_element_type=F32)


def local_grads(normed, patches, attention, upstream, values, output_b):
    mixed = apply_heads(attention, values)
    outcome = patches.astype(F32) + jnp.dot(mixed, output_b, preferred_element_type=F32)
    centred = outcome - jnp.mean(outcome, axis=-1, keepdims=True)
    inverse = lax.rsqrt(jnp.mean(centred * centred, axis=-1, keepdims=True) + 1e-06)
    normal_out = centred * inverse
    signal = upstream.astype(F32)
    d_outcome = inverse * (
        signal
        - jnp.mean(signal, axis=-1, keepdims=True)
        - normal_out * jnp.mean(signal * normal_out, axis=-1, keepdims=True)
    )
    d_outcome = d_outcome.astype(BF)
    grad_output = contract_rows(mixed, d_outcome)
    d_mixed = lax.dot_general(
        d_outcome, output_b, (((1,), (1,)), ((), ())), preferred_element_type=F32
    ).astype(BF)
    d_values = apply_back(attention, d_mixed)
    grad_value = contract_rows(normed, d_values)
    return grad_value.astype(BF), grad_output.astype(BF)


def fold_output(rows, lead):
    half = rows.reshape(lead + (56, 2, HID))
    return jnp.swapaxes(half, -3, -2).reshape(lead + (BLOCKS, 16, HID))


def unfold_output(blocks):
    folded = blocks.reshape(-1, 2, 56, HID)
    return jnp.swapaxes(folded, 1, 2).reshape(-1, D)


def pack(grad_value, grad_output):
    value = grad_value.reshape(2, 4, 2, BLOCKS, 16, HID)
    output = fold_output(grad_output, (2, 4, 2))
    both = jnp.concatenate([value, output], axis=0)
    return both[..., :WIDTHS[0]], both[..., WIDTHS[0]:]


def unpack(fulls):
    both = jnp.concatenate(fulls, axis=-1)
    return both[:2].reshape(D, HID), unfold_output(both[2:])


def adam_update(weight, first, second, gradient):
    first_new = beta_one * first + (1.0 - beta_one) * gradient
    second_new = beta_two * second + (1.0 - beta_two) * gradient * gradient
    update = (
        first_new / first_fix / (jnp.sqrt(second_new / second_fix) + adam_eps)
        + weight_decay * weight
    )
    return (weight - learn_rate * update, first_new, second_new)


def on_device(
    patches,
    queries,
    keys,
    upstream,
    value_weight,
    output_weight,
    value_first,
    output_first,
    value_second,
    output_second,
):
    own = jnp.stack([
        value_weight.astype(BF).reshape(BLOCKS, 16, HID),
        fold_output(output_weight.astype(BF), ()),
    ])
    value_full, output_full = unpack(gather_weights(own))
    normed = norm_rows(patches).astype(BF)
    attention = attention_weights(queries, keys)
    base = jnp.dot(normed, value_full, preferred_element_type=F32)
    grads = local_grads(normed, patches, attention, upstream, base.astype(BF), output_full)
    value_sum, output_sum = unpack(sum_and_gather(pack(*grads)))
    squares = jnp.sum(value_sum.astype(F32) ** 2) + jnp.sum(output_sum.astype(F32) ** 2)
    stretch = rho_scale / jnp.sqrt(squares / (2.0 * D * HID) + 1e-06)
    values = base + stretch * jnp.dot(normed, value_sum, preferred_element_type=F32)
    output_shifted = (output_full.astype(F32) + stretch * output_sum.astype(F32)).astype(BF)
    grads = local_grads(normed, patches, attention, upstream, values.astype(BF), output_shifted)
    owned = jnp.concatenate(sum_owned(pack(*grads)), axis=-1).astype(F32)
    value_new, value_first_new, value_second_new = adam_update(
        value_weight, value_first, value_second, owned[0].reshape(112, HID)
    )
    output_new, output_first_new, output_second_new = adam_update(
        output_weight, output_first, output_second, unfold_output(owned[1])
    )
    return (
        value_new,
        output_new,
        value_first_new,
        output_first_new,
        value_second_new,
        output_second_new,
    )


def solution(mesh):
    return jax.shard_map(
        on_device,
        mesh=mesh,
        in_specs=(P(("dp", "fsdp"), None),) * 4 + (P("fsdp", None),) * 6,
        out_specs=(P("fsdp", None),) * 6,
        check_vma=False,
    )
```

time: 917 us -> 307 us (0.33)
  waiting for transfers between devices: 813 us -> 0 us
  Pallas kernels: 0 us -> 168 us
  local copies, waits for them, and re-layouts: 2.99 us -> 63.3 us
  blocking collectives: 28.3 us -> 0 us
  other arithmetic: 17.6 us -> 36 us
  between operations: 16.4 us -> 2.63 us
    reduce_scatter x4 -> x0, waiting for transfers between devices: 327 us -> none  [the longest x2 176 us: combine(): lax.psum_scatter(gradient_pair[0].astype(jnp.bfloat16), 'fsdp', scatter_d...]
    psum x2 -> x0, waiting for transfers between devices: 269 us -> none  [the longest x1 134 us: combine(): lax.psum(owned[0].astype(jnp.bfloat16), 'dp').astype(jnp.float32)]
    all_gather x4 -> x0, waiting for transfers between devices: 218 us -> none  [the longest x2 109 us: gradients(): lax.all_gather(output_owned, 'fsdp', axis=0, tiled=True)]
    pallas_call x0 -> x3, Pallas kernels: none -> 168 us  [the longest x1 74.2 us: sum_and_gather(): pl.pallas_call(middle_kernel, out_shape=full_shapes(), in_specs=vmem(2),...]
    psum x1 -> x0, blocking collectives: 28.3 us -> none  [combine(): squares = lax.psum(local_sq, 'fsdp')]
    reshape x0 -> x6, local copies, waits for them, and re-layouts: none -> 23.8 us  [the longest x5 19.4 us: fold_output(): half = rows.reshape(lead + (56, 2, HID))]
    unnamed x34 -> x58, local copies, waits for them, and re-layouts: 2.14 us -> 18.6 us
  transfers between devices with their start and end apart: 10 -> 0, of which waited for: 10 -> 0; matrix products, arithmetic and copies ran while one was open for 4% -> 0% of each run, Pallas kernels for 0% -> 0%
where the time goes in v1:
time: 307 us; the launch traced here: 303 us
  Pallas kernels  168 us (55%)
  local copies, waits for them, and re-layouts  63.3 us (21%)
  other arithmetic  36 us (12%)
  matrix products  34 us (11%)
    pallas_call x1, Pallas kernels, sum_and_gather(): pl.pallas_call(middle_kernel, out_shape=full_shapes(), in_specs=vmem(2),...  74.2 us
    pallas_call x1, Pallas kernels, sum_owned(): pl.pallas_call(last_kernel, out_shape=tuple((jax.ShapeDtypeStruct((2, BLO...  54.2 us
    pallas_call x1, Pallas kernels, gather_weights(): pl.pallas_call(weights_kernel, out_shape=full_shapes(), in_specs=vmem(2),...  39.2 us
    reshape x5, local copies, waits for them, and re-layouts, fold_output(): half = rows.reshape(lead + (56, 2, HID))  19.4 us
    unnamed x58, local copies, waits for them, and re-layouts  18.6 us
    dot_general x4, matrix products, contract_rows(): lax.dot_general(left, right, (((0,), (0,)), ((), ())), preferred_element_...  10.7 us
    mul x1, local copies, waits for them, and re-layouts, on_device(): stretch * output_sum.astype(F32)  8.81 us
    convert_element_type x1, other arithmetic, on_device(): (output_full.astype(F32) + stretch * output_sum.astype(F32)).astype(BF)  8.72 us

profile of v1, /device:TPU:8, one launch (start us, length us, event | category | flops | bytes accessed | tf_op | source)
XLA Modules:
  0.0 303.5 jit_solution(5257003194060841508)
XLA Ops:
  0.7 1.5 convert_reduce_fusion.1
  2.1 1.6 fusion.15
  3.7 1.0 convert_element_type.140
  4.7 1.0 convert_element_type.141
  6.5 0.7 fusion.26.own_a
  7.6 2.2 fusion.45
  9.8 1.8 divide_convert_fusion
  11.6 39.2 %gather_weights.1 = (bf16[4,4,2,7,16,512]{5,4,3,2,1,0:T(8,128)(2,1)}, bf16[4,4,2,7,16,384]{5,4,3,2,1,0:T(8,128)(2,1)}) custom-call(bf16[2,7,16,512]{3,2,1,0:T(8,128)(2,1)} %fusion.26.own_a, bf16[2,7,16,384]{3,2,1,0:T(8,128)(2,1)} %pad_maximum_fusion.2.own_b), custom_call_target="tpu_custom_call" | custom-call | tf_op jit(solution)/shard_map/gather_weights/pallas_call | solution.py:434
  50.8 2.6 constant_dynamic-update-slice_fusion.1
  54.3 2.2 fusion.42
  56.5 2.1 fusion.44
  59.2 4.4 %copy.35 = bf16[16,2,56,896]{3,1,2,0:T(2,128)(2,1)S(1)} copy(bf16[16,2,56,896]{3,2,1,0:T(8,128)(2,1)} %bitcast.108) | data formatting | bytes 6422528 | tf_op jit(solution)/shard_map/reshape | solution.py:538
  64.2 1.2 fusion.46
  66.6 2.1 convolution_convert_fusion.4
  68.7 2.0 copy.36
  70.7 2.6 convolution_convert_fusion.7
  73.4 4.1 %convolution_convert_fusion.2 = bf16[896,1792]{1,0:T(8,128)(2,1)} fusion(bf16[256,896]{0,1:T(8,128)(2,1)S(1)} %bitcast.116, bf16[256,1792]{1,0:T(8,128)(2,1)} %param.13, f32[256,1792]{1,0:T(8,128)S(1)} %get-tuple-element.37, f32[256]{0:T(256)S(1)} %get-tuple-element.40, f32[256]{0:T(256)S(1)} %get-tuple-element.41, f32[256]{0:T(256)S(1)} %add_rsqrt_fusion.1, ...), kind=kOutput, calls=%fused_computation.16 | convolution fusion | flops 827359232 | bytes 6426624 | tf_op jit(solution)/shard_map/dot_general | solution.py:507
  77.4 7.6 %reshape.192 = bf16[2,4,2,56,2,896]{5,4,3,2,1,0:T(2,128)(2,1)} reshape(bf16[896,1792]{1,0:T(8,128)(2,1)} %convolution_convert_fusion.2) | data formatting | bytes 6422528 | tf_op jit(solution)/shard_map/reshape | solution.py:533
  85.0 2.4 copy.38
  87.4 1.3 convolution_convert_fusion.3
  88.7 1.8 pad_maximum_fusion.1.grad_b
  90.5 2.0 fusion.4.grad_a
  92.5 74.2 %sum_and_gather.1 = (bf16[4,4,2,7,16,512]{5,4,3,2,1,0:T(8,128)(2,1)}, bf16[4,4,2,7,16,384]{5,4,3,2,1,0:T(8,128)(2,1)}) custom-call(bf16[4,4,2,7,16,512]{5,4,3,2,1,0:T(8,128)(2,1)} %fusion.4.grad_a, bf16[4,4,2,7,16,384]{5,4,3,2,1,0:T(8,128)(2,1)} %pad_maximum_fusion.1.grad_b), custom_call_target="tpu_custom_call" | custom-call | tf_op jit(solution)/shard_map/sum_and_gather/pallas_call | solution.py:454
  166.8 2.6 constant_dynamic-update-slice_fusion.3
  170.2 2.6 fusion.1
  174.3 4.0 %slice.54 = bf16[2,4,2,7,16,896]{5,4,3,2,1,0:T(8,128)(2,1)} slice(bf16[4,4,2,7,16,896]{5,4,3,2,1,0:T(8,128)(2,1)} %copy-done), slice={[0:2], [0:4], [0:2], [0:7], [0:16], [0:896]} | slice | bytes 6422528 | tf_op jit(solution)/shard_map/slice | solution.py:551
  178.2 1.0 copy-done.1
  179.2 3.3 %convert_multiply_fusion = f32[2,4,2,7,16,896]{5,4,3,2,1,0:T(8,128)} fusion(f32[]{:T(128)S(6)} %div.82, bf16[4,4,2,7,16,896]{5,4,3,2,1,0:T(8,128)(2,1)S(1)} %copy-done.1), kind=kLoop, calls=%fused_computation.1 | loop fusion | flops 3211264 | bytes 9633796 | tf_op jit(solution)/shard_map/mul | solution.py:589
  182.5 8.7 %fusion.2 = bf16[16,56,2,896]{3,2,1,0:T(2,128)(2,1)} fusion(f32[16,2,56,896]{3,2,1,0:T(8,128)} %bitcast.95, bf16[16,2,56,896]{3,2,1,0:T(8,128)(2,1)S(1)} %bitcast.109), kind=kLoop, calls=%fused_computation.9 | loop fusion | flops 4816896 | bytes 12845056 | tf_op jit(solution)/shard_map/convert_element_type | solution.py:589
  191.3 8.8 %copy.41 = f32[16,2,56,896]{3,1,2,0:T(2,128)} copy(f32[16,2,56,896]{3,2,1,0:T(8,128)} %bitcast.96) | data formatting | bytes 12845056 | tf_op jit(solution)/shard_map/mul | solution.py:589
  200.1 6.1 %copy.53 = f32[112,8,2,896]{3,1,2,0:T(8,128)} copy(f32[112,8,2,896]{3,2,1,0:T(2,128)} %bitcast.111) | data formatting | bytes 12845056
  206.2 2.3 copy.52
  209.5 1.2 fusion.20
  211.2 3.4 %fusion.47 = (f32[256]{0:T(256)S(1)}, f32[256,1792]{1,0:T(8,128)S(1)}) fusion(bf16[256,896]{0,1:T(8,128)(2,1)S(1)} %bitcast.117, bf16[896,1792]{1,0:T(8,128)(2,1)} %bitcast.112, bf16[256,1792]{1,0:T(8,128)(2,1)S(1)} %copy-done.2), kind=kOutput, calls=%fused_computation.93 | convolution fusion | flops 823459584 | bytes 6423552 | tf_op jit(solution)/shard_map/dot_general | solution.py:512
  215.5 1.1 copy-done.4
  216.6 5.2 %fusion.21 = bf16[256,896]{1,0:T(8,128)(2,1)} fusion(f32[896,1792]{1,0:T(8,128)} %bitcast.110, bf16[896,1792]{1,0:T(8,128)(2,1)S(1)} %bitcast.107, bf16[256,1792]{1,0:T(8,128)(2,1)S(1)} %copy-done.9, f32[256,1792]{1,0:T(8,128)S(1)} %get-tuple-element.39, f32[256]{0:T(256)S(1)} %broadcast_multiply_fusion, f32[256]{0:T(256)S(1)} %add_rsqrt_fusion, ...), kind=kOutput, calls=%fused_computation.55 | convolution fusion | flops 830799872 | bytes 12849152 | tf_op jit(solution)/shard_map/dot_general | solution.py:524
  221.7 2.0 copy.42
  223.7 2.6 convolution_convert_fusion.5
  226.3 4.1 %convolution_convert_fusion = bf16[896,1792]{1,0:T(8,128)(2,1)} fusion(bf16[256,896]{0,1:T(8,128)(2,1)S(1)} %bitcast.118, bf16[256,1792]{1,0:T(8,128)(2,1)} %param.13, f32[256,1792]{1,0:T(8,128)S(1)} %get-tuple-element.39, f32[256]{0:T(256)S(1)} %broadcast_multiply_fusion, f32[256]{0:T(256)S(1)} %add_rsqrt_fusion, f32[256]{0:T(256)S(1)} %broadcast_multiply_fusion.1, ...), kind=kOutput, calls=%fused_computation.14 | convolution fusion | flops 827359232 | bytes 6426624 | tf_op jit(solution)/shard_map/dot_general | solution.py:507
  230.4 7.1 %reshape.198 = bf16[2,4,2,56,2,896]{5,4,3,2,1,0:T(2,128)(2,1)} reshape(bf16[896,1792]{1,0:T(8,128)(2,1)} %convolution_convert_fusion) | data formatting | bytes 6422528 | tf_op jit(solution)/shard_map/reshape | solution.py:533
  237.5 2.4 copy.44
  239.8 1.3 convolution_convert_fusion.1
  241.1 1.8 pad_maximum_fusion.grad_b
  243.0 2.0 fusion.3.grad_a
  245.0 54.2 %sum_owned.1 = (bf16[2,7,16,512]{3,2,1,0:T(8,128)(2,1)}, bf16[2,7,16,384]{3,2,1,0:T(8,128)(2,1)}) custom-call(bf16[4,4,2,7,16,512]{5,4,3,2,1,0:T(8,128)(2,1)} %fusion.3.grad_a, bf16[4,4,2,7,16,384]{5,4,3,2,1,0:T(8,128)(2,1)} %pad_maximum_fusion.grad_b), custom_call_target="tpu_custom_call" | custom-call | tf_op jit(solution)/shard_map/sum_owned/pallas_call | solution.py:466
  299.3 1.2 maximum_convert_fusion
  300.8 1.2 multiply_subtract_fusion
  302.0 1.2 multiply_subtract_fusion.1
  (74 shorter events, 7.8 us)
Async XLA Ops:
  0.6 6.8 %copy-start.19 = (bf16[256,896]{1,0:T(8,128)(2,1)S(1)}, bf16[256,896]{1,0:T(8,128)(2,1)}, u32[]{:S(2)}) copy-start(bf16[256,896]{1,0:T(8,128)(2,1)} %param.12) | copy-start | bytes 1376260
  0.6 6.5 %copy-start.18 = (bf16[256,896]{1,0:T(8,128)(2,1)S(1)}, bf16[256,896]{1,0:T(8,128)(2,1)}, u32[]{:S(2)}) copy-start(bf16[256,896]{1,0:T(8,128)(2,1)} %param.11) | copy-start | bytes 1376260
  11.6 47.3 %copy-start.6 = (bf16[8,256,256]{1,2,0:T(8,128)(2,1)}, bf16[8,256,256]{1,2,0:T(8,128)(2,1)S(1)}, u32[]{:S(2)}) copy-start(bf16[8,256,256]{1,2,0:T(8,128)(2,1)S(1)} %divide_convert_fusion) | copy-start | bytes 3145732
  50.8 2.9 copy-start.12
  54.3 2.2 copy-start.2
  64.1 2.4 copy-start.3
  64.2 1.9 copy-start.8
  85.0 2.4 copy-start.15
  166.7 2.9 copy-start.13
  170.2 2.7 copy-start
  174.2 4.9 %copy-start.1 = (bf16[4,4,2,7,16,896]{5,4,3,2,1,0:T(8,128)(2,1)S(1)}, bf16[4,4,2,7,16,896]{5,4,3,2,1,0:T(8,128)(2,1)}, u32[]{:S(2)}) copy-start(bf16[4,4,2,7,16,896]{5,4,3,2,1,0:T(8,128)(2,1)} %copy-done) | copy-start | bytes 19267588
  179.2 3.4 %copy-start.5 = (bf16[2,4,2,7,16,896]{5,4,3,2,1,0:T(8,128)(2,1)S(1)}, bf16[2,4,2,7,16,896]{5,4,3,2,1,0:T(8,128)(2,1)}, u32[]{:S(2)}) copy-start(bf16[2,4,2,7,16,896]{5,4,3,2,1,0:T(8,128)(2,1)} %get-tuple-element.29) | copy-start | bytes 9633796
  200.1 6.1 %copy-start.10 = (bf16[16,56,2,896]{3,2,1,0:T(2,128)(2,1)S(1)}, bf16[16,56,2,896]{3,2,1,0:T(2,128)(2,1)}, u32[]{:S(2)}) copy-start(bf16[16,56,2,896]{3,2,1,0:T(2,128)(2,1)} %fusion.2) | copy-start | bytes 9633796
  206.2 2.9 copy-start.11
  206.2 3.3 %copy-start.24 = (f32[256,896]{1,0:T(8,128)S(1)}, f32[256,896]{1,0:T(8,128)}, u32[]{:S(2)}) copy-start(f32[256,896]{1,0:T(8,128)} %get-tuple-element.33) | copy-start | bytes 2752516
  209.5 1.4 copy-start.7
  211.2 3.8 %copy-start.9 = (bf16[256,1792]{1,0:T(8,128)(2,1)S(1)}, bf16[256,1792]{1,0:T(8,128)(2,1)}, u32[]{:S(2)}) copy-start(bf16[256,1792]{1,0:T(8,128)(2,1)} %param.13) | copy-start | bytes 2752516
  214.6 1.9 copy-start.4
  237.5 2.4 copy-start.14
  299.2 1.6 copy-start.16
  299.2 1.6 copy-start.20
  299.2 1.6 copy-start.21
  300.4 1.6 copy-start.17
  300.4 1.6 copy-start.22
  300.5 1.6 copy-start.23

commit v2 on v1

--- a/solution.py
+++ b/solution.py
@@ -1,5 +1,3 @@
-import functools
-
 import jax
 import jax.numpy as jnp
 from jax import lax
@@ -119,11 +117,11 @@
     return shapes
 
 
-def reduce_all(net, grads, outs, scratch):
+def reduce_all(net, grads, outs, scratch, make):
+    make(1 - net.c)
     state = []
     for part in (0, 1):
         state.append(scratch[part * 9:part * 9 + 9])
-    rows = []
     cores = [[], []]
     for step in (2, 1, 3, 0):
         for part in (0, 1):
@@ -136,7 +134,7 @@
             else:
                 src, dst = grads[part].at[:, i, 1 - net.c], other.at[:, i]
             cores[part].append(push(src, dst, sem.at[0, j], sem.at[1, j], net.core()))
-    waits = []
+    make(net.c)
 
     def half_of(ref, part, i, h):
         return ref.at[i, pl.ds(2 * h, 2)] if part == 0 else ref.at[pl.ds(2 * h, 2), i]
@@ -258,7 +256,7 @@
     return [pltpu.SemaphoreType.DMA((2, 3 + 6 + 8)) for _ in WIDTHS]
 
 
-def gather_all(net, fulls, sems):
+def gather_all(net, fulls, sems, between=()):
     seconds = [[], []]
     for part in (0, 1):
         second = ordered(part)[1]
@@ -276,6 +274,8 @@
 
     copies = [[], []]
     cores = [[], []]
+    if between:
+        between[0]()
     for part in (0, 1):
         first = ordered(part)[0]
         for copy in seconds[part]:
@@ -286,6 +286,8 @@
         for j, (h, to) in enumerate(((0, right), (1, left), (1, right), (0, left))):
             copies[part].append(push(line(part, me, h), line(part, me, h), sem.at[0, 3 + j], sem.at[1, 3 + j], to))
         cores[part].append(push(whole(part, me), whole(part, me), sem.at[0, 9], sem.at[1, 9], net.core()))
+    if between:
+        between[1]()
     for part in (0, 1):
         first = ordered(part)[0]
         right, left = net.along(first, 1), net.along(first, 3)
@@ -311,17 +313,6 @@
             copy.wait_send()
 
 
-def weights_kernel(own_a, own_b, full_a, full_b, sem_a, sem_b, copy_sem):
-    net = Net()
-    net.barrier()
-    fulls = (full_a, full_b)
-    for part, own in enumerate((own_a, own_b)):
-        copy = pltpu.make_async_copy(own.at[net.x % 2], fulls[part].at[net.spot("x"), net.spot("y"), net.c], copy_sem.at[part])
-        copy.start()
-        copy.wait()
-    gather_all(net, fulls, (sem_a, sem_b))
-
-
 def spread_line(net, fulls, outs, sems):
     for part in (0, 1):
         @pl.when(net.z != 7)
@@ -350,23 +341,7 @@
                     copy.wait_send()
 
 
-def middle_kernel(grad_a, grad_b, full_a, full_b, out_a, out_b, line_a, line_b, sem_a, sem_b, *scratch):
-    net = Net()
-    net.barrier()
-    fulls, outs = (full_a, full_b), (out_a, out_b)
-    drain = reduce_all(net, (grad_a, grad_b), outs, scratch)
-    spread_line(net, fulls, outs, (line_a, line_b))
-    wait_line(net, fulls, (line_a, line_b), True)
-    gather_all(net, fulls, (sem_a, sem_b))
-    wait_line(net, fulls, (line_a, line_b), False)
-    drain()
-
-
-def last_kernel(grad_a, grad_b, owned_a, owned_b, out_a, out_b, line_a, line_b, pair_a, pair_b, *scratch):
-    net = Net()
-    net.barrier()
-    owned, outs = (owned_a, owned_b), (out_a, out_b)
-    drain = reduce_all(net, (grad_a, grad_b), outs, scratch)
+def share_owned(net, outs, owned, sems, pairs):
     half = net.x % 2
     partner = device(net.x + 1 - 2 * half, net.y, net.z, net.c)
 
@@ -374,17 +349,15 @@
         return owned[part].at[half, jnp.minimum(z, 6)]
 
     def line_copy(part, d, z):
-        sems = (line_a, line_b)[part]
         return pltpu.make_async_remote_copy(
-            src_ref=block(part, z), dst_ref=block(part, z), send_sem=sems.at[0, d - 1], recv_sem=sems.at[1, d - 1],
-            device_id=net.along("z", d), device_id_type=MESH,
+            src_ref=block(part, z), dst_ref=block(part, z), send_sem=sems[part].at[0, d - 1],
+            recv_sem=sems[part].at[1, d - 1], device_id=net.along("z", d), device_id_type=MESH,
         )
 
     def pair_copy(part, d, z):
-        sems = (pair_a, pair_b)[part]
         return pltpu.make_async_remote_copy(
-            src_ref=block(part, z), dst_ref=block(part, z), send_sem=sems.at[0, d], recv_sem=sems.at[1, d],
-            device_id=partner, device_id_type=MESH,
+            src_ref=block(part, z), dst_ref=block(part, z), send_sem=pairs[part].at[0, d],
+            recv_sem=pairs[part].at[1, d], device_id=partner, device_id_type=MESH,
         )
 
     for part in (0, 1):
@@ -414,141 +387,258 @@
         def _():
             for d in range(1, 8):
                 line_copy(part, d, net.z).wait_send()
+
+
+def loop(count, body):
+    def step(i, carry):
+        body(i)
+        return carry
+
+    lax.fori_loop(0, count, step, 0)
+
+
+STARTS = (0, WIDTHS[0])
+
+
+def norm_patches(patches, normed, normed_t):
+    def norm(i):
+        at = pl.ds(pl.multiple_of(i * 32, 32), 32)
+        rows = patches[at, :].astype(F32)
+        centred = rows - jnp.mean(rows, axis=-1, keepdims=True)
+        scale = lax.rsqrt(jnp.mean(centred * centred, axis=-1, keepdims=True) + 1e-06)
+        normed[at, :] = (centred * scale).astype(BF)
+
+    loop(8, norm)
+
+    def turn(j):
+        block = normed[:, pl.ds(pl.multiple_of(j * 128, 128), 128)]
+        normed_t[pl.ds(j * 8, 8)] = block.T.reshape(8, 16, SEQ)
+
+    loop(14, turn)
+
+
+def attend(queries, keys, attention, attention_t):
+    for h in range(HEADS):
+        q = queries[:, h * HD:(h + 1) * HD]
+        k = keys[:, h * HD:(h + 1) * HD]
+        scores = lax.dot_general(q, k, (((1,), (1,)), ((), ())), preferred_element_type=F32) * HD ** (-0.5)
+        expo = jnp.exp(scores - jnp.max(scores, axis=-1, keepdims=True))
+        weights = (expo / jnp.sum(expo, axis=-1, keepdims=True)).astype(BF)
+        attention[h] = weights
+        attention_t[h] = weights.T
+
+
+def project(normed, fulls, write):
+    for part in (0, 1):
+        w, at = WIDTHS[part], STARTS[part]
+        total = jnp.dot(normed[:, :HID], fulls[part][0].reshape(HID, w), preferred_element_type=F32)
+        total = total + jnp.dot(normed[:, HID:], fulls[part][1].reshape(HID, w), preferred_element_type=F32)
+        write(slice(at, at + w), total)
+
+
+def unfold(full, i):
+    both = full[2 + i // 4, i % 4].astype(F32)
+    both = both.reshape(2, 112, both.shape[-1])
+    left = jnp.concatenate([both[0, :56], both[1, :56]], axis=0)
+    right = jnp.concatenate([both[0, 56:], both[1, 56:]], axis=0)
+    return left, right
+
+
+def set_output(fulls, output, stretch):
+    def step(i):
+        for part in (0, 1):
+            w = WIDTHS[part]
+            for half, rows in enumerate(unfold(fulls[part], i)):
+                at = (pl.ds(i * BLOCKS, BLOCKS), slice(None), slice(half * HID + STARTS[part], half * HID + STARTS[part] + w))
+                if stretch is not None:
+                    rows = output[at].astype(F32).reshape(112, w) + stretch * rows
+                output[at] = rows.astype(BF).reshape(BLOCKS, 16, w)
+
+    loop(8, step)
+
+
+def sum_squares(fulls):
+    def step(i, totals):
+        out = []
+        for part in (0, 1):
+            block = fulls[part][i // 4, i % 4].astype(F32)
+            block = block.reshape(2 * BLOCKS, 16, WIDTHS[part])
+            out.append(totals[part] + jnp.sum(block * block, axis=0))
+        return tuple(out)
+
+    totals = lax.fori_loop(0, 16, step, tuple(jnp.zeros((16, w), F32) for w in WIDTHS))
+    parts = [jnp.sum(jnp.sum(t, axis=0, keepdims=True), axis=1, keepdims=True) for t in totals]
+    return parts[0] + parts[1]
+
+
+def backward(patches, upstream, attention, attention_t, output, values, mixed, mixed_t, outcome, d_outcome, d_values):
+    for h in range(HEADS):
+        at = slice(h * HD, (h + 1) * HD)
+        mixed[:, at] = jnp.dot(attention[h], values[:, at], preferred_element_type=F32).astype(BF)
+
+    def turn(j):
+        block = mixed[:, pl.ds(pl.multiple_of(j * 128, 128), 128)].astype(F32)
+        mixed_t[pl.ds(j * 16, 16)] = block.T.reshape(16, 8, SEQ)
+
+    loop(7, turn)
+
+    def columns(n):
+        at = pl.ds(pl.multiple_of(n * 256, 256), 256)
+        outcome[:, at] = patches[:, at].astype(F32) + jnp.dot(
+            mixed[...], output[:, :, at].reshape(HID, 256), preferred_element_type=F32
+        )
+
+    loop(7, columns)
+
+    def rows(i):
+        at = pl.ds(pl.multiple_of(i * 32, 32), 32)
+        total = outcome[at, :]
+        centred = total - jnp.mean(total, axis=-1, keepdims=True)
+        inverse = lax.rsqrt(jnp.mean(centred * centred, axis=-1, keepdims=True) + 1e-06)
+        normal = centred * inverse
+        signal = upstream[at, :].astype(F32)
+        grad = inverse * (
+            signal
+            - jnp.mean(signal, axis=-1, keepdims=True)
+            - normal * jnp.mean(signal * normal, axis=-1, keepdims=True)
+        )
+        d_outcome[at, :] = grad.astype(BF)
+
+    loop(8, rows)
+    d_mixed = lax.dot_general(
+        d_outcome[...], output[...].reshape(HID, D), (((1,), (1,)), ((), ())), preferred_element_type=F32
+    ).astype(BF)
+    values[...] = d_mixed
+    for h in range(HEADS):
+        at = slice(h * HD, (h + 1) * HD)
+        d_values[:, at] = jnp.dot(attention_t[h], values[:, at], preferred_element_type=F32).astype(BF)
+
+
+def write_grads(core, normed_t, mixed_t, d_outcome, d_values, grads):
+    for hi in (0, 1):
+        rows = [mixed_t[pl.ds((hi * 8 + y * 2 + core) * BLOCKS, BLOCKS)].reshape(56, SEQ) for y in range(4)]
+        left = jnp.concatenate(rows, axis=0).astype(BF)
+        got = jnp.dot(left, d_outcome[...], preferred_element_type=F32).reshape(4, 56, D)
+        got = jnp.concatenate([got[:, :, :HID], got[:, :, HID:]], axis=1).astype(BF).reshape(4, BLOCKS, 16, HID)
+        for part in (0, 1):
+            grads[part][2 + hi, :, core] = got[..., STARTS[part]:STARTS[part] + WIDTHS[part]]
+    for hi in (0, 1):
+        rows = [normed_t[pl.ds((hi * 8 + y * 2 + core) * BLOCKS, BLOCKS)] for y in range(4)]
+        left = jnp.concatenate(rows, axis=0).reshape(448, SEQ)
+        got = jnp.dot(left, d_values[...], preferred_element_type=F32).astype(BF).reshape(4, BLOCKS, 16, HID)
+        for part in (0, 1):
+            grads[part][hi, :, core] = got[..., STARTS[part]:STARTS[part] + WIDTHS[part]]
+
+
+def kernel(
+    patches, queries, keys, upstream, own,
+    value_grad, output_grad,
+    full_a, full_b, grad_a, grad_b, owned_a, owned_b,
+    normed, normed_t, attention, attention_t, base, values, output,
+    mixed, mixed_t, outcome, d_outcome, d_values,
+    sem_a, sem_b, again_a, again_b, out_a, out_b, line_a, line_b, last_a, last_b, pair_a, pair_b, *scratch,
+):
+    net = Net()
+    net.barrier()
+    fulls, grads, outs, owned = (full_a, full_b), (grad_a, grad_b), (out_a, out_b), (owned_a, owned_b)
+    for part in (0, 1):
+        fulls[part][net.spot("x"), net.spot("y"), net.c] = own[net.x % 2, :, :, STARTS[part]:STARTS[part] + WIDTHS[part]]
+    gather_all(
+        net, fulls, (sem_a, sem_b),
+        (lambda: norm_patches(patches, normed, normed_t), lambda: attend(queries, keys, attention, attention_t)),
+    )
+    set_output(fulls, output, None)
+
+    def write_base(at, total):
+        base[:, at] = total
+        values[:, at] = total.astype(BF)
+
+    project(normed, fulls, write_base)
+
+    def back():
+        backward(patches, upstream, attention, attention_t, output, values, mixed, mixed_t, outcome, d_outcome, d_values)
+
+    def make(core):
+        write_grads(core, normed_t, mixed_t, d_outcome, d_values, grads)
+
+    back()
+    drain = reduce_all(net, grads, outs, scratch, make)
+    spread_line(net, fulls, outs, (line_a, line_b))
+    wait_line(net, fulls, (line_a, line_b), True)
+    gather_all(net, fulls, (again_a, again_b))
+    wait_line(net, fulls, (line_a, line_b), False)
     drain()
+    mean_square = sum_squares(fulls) / (2.0 * D * HID)
+    stretch = rho_scale / jnp.sqrt(mean_square + 1e-06)
+    set_output(fulls, output, stretch)
+
+    def write_values(at, total):
+        values[:, at] = (base[:, at] + stretch * total).astype(BF)
+
+    project(normed, fulls, write_values)
+    back()
+    drain = reduce_all(net, grads, outs, scratch, make)
+    share_owned(net, outs, owned, (last_a, last_b), (pair_a, pair_b))
+    drain()
+    for part in (0, 1):
+        w, at = WIDTHS[part], STARTS[part]
+        value_grad[:, :, at:at + w] = owned[part][0]
+        rows = owned[part][1].astype(F32).reshape(112, w)
+        output_grad[:, at:at + w] = rows[:56]
+        output_grad[:, HID + at:HID + at + w] = rows[56:]
 
 
 def vmem(n):
     return [pl.BlockSpec(memory_space=pltpu.VMEM)] * n
 
 
-def params(cid):
-    return pltpu.CompilerParams(collective_id=cid, has_side_effects=True, vmem_limit_bytes=60 * 2**20)
-
-
-def full_shapes():
-    return tuple(jax.ShapeDtypeStruct((4, 4, 2, BLOCKS, 16, w), BF) for w in WIDTHS)
-
-
-def gather_weights(own):
-    a, b = own[..., :WIDTHS[0]], own[..., WIDTHS[0]:]
-    return pl.pallas_call(
-        weights_kernel,
-        out_shape=full_shapes(),
-        in_specs=vmem(2),
-        out_specs=vmem(2),
-        scratch_shapes=gather_scratch() + [pltpu.SemaphoreType.DMA((2,))],
-        name="gather_weights",
-        compiler_params=params(0),
-    )(a, b)
-
-
 def line_sems(n=7):
     return [pltpu.SemaphoreType.DMA((2, n)) for _ in WIDTHS]
 
 
-def block_scratch():
-    return [pltpu.VMEM((16, w), BF) for w in WIDTHS]
-
-
-def sum_and_gather(grads):
+def gradients(patches, queries, keys, upstream, own):
+    rows = patches.shape[0]
     return pl.pallas_call(
-        middle_kernel,
-        out_shape=full_shapes(),
-        in_specs=vmem(2),
+        kernel,
+        out_shape=(
+            jax.ShapeDtypeStruct((BLOCKS, 16, HID), BF),
+            jax.ShapeDtypeStruct((56, D), F32),
+        ),
+        in_specs=vmem(5),
         out_specs=vmem(2),
-        scratch_shapes=block_scratch() + line_sems() + gather_scratch() + reduce_scratch(),
-        name="sum_and_gather",
-        compiler_params=params(1),
-    )(*grads)
-
-
-def sum_owned(grads):
-    return pl.pallas_call(
-        last_kernel,
-        out_shape=tuple(jax.ShapeDtypeStruct((2, BLOCKS, 16, w), BF) for w in WIDTHS),
-        in_specs=vmem(2),
-        out_specs=vmem(2),
-        scratch_shapes=block_scratch() + line_sems() + line_sems(8) + reduce_scratch(),
-        name="sum_owned",
-        compiler_params=params(2),
-    )(*grads)
-
-
-def norm_rows(rows):
-    rows = rows.astype(F32)
-    centred = rows - jnp.mean(rows, axis=-1, keepdims=True)
-    return centred * lax.rsqrt(jnp.mean(centred * centred, axis=-1, keepdims=True) + 1e-06)
-
-
-def attention_weights(queries, keys):
-    query_heads = queries.reshape(-1, SEQ, HEADS, HD)
-    key_heads = keys.reshape(-1, SEQ, HEADS, HD)
-    scores = jnp.einsum("bqhd,bkhd->bhqk", query_heads, key_heads, preferred_element_type=F32) * HD ** (-0.5)
-    scores = scores - jnp.max(scores, axis=-1, keepdims=True)
-    expo = jnp.exp(scores)
-    return (expo / jnp.sum(expo, axis=-1, keepdims=True)).astype(BF)
-
-
-def apply_heads(attention, values):
-    rows = values.shape[0]
-    heads = values.reshape(-1, SEQ, HEADS, HD)
-    mixed = jnp.einsum("bhqk,bkhd->bqhd", attention, heads, preferred_element_type=F32)
-    return mixed.reshape(rows, HEADS * HD).astype(BF)
-
-
-def apply_back(attention, d_mixed):
-    rows = d_mixed.shape[0]
-    heads = d_mixed.reshape(-1, SEQ, HEADS, HD)
-    back = jnp.einsum("bhqk,bqhd->bkhd", attention, heads, preferred_element_type=F32)
-    return back.reshape(rows, HEADS * HD).astype(BF)
-
-
-def contract_rows(left, right):
-    return lax.dot_general(left, right, (((0,), (0,)), ((), ())), preferred_element_type=F32)
-
-
-def local_grads(normed, patches, attention, upstream, values, output_b):
-    mixed = apply_heads(attention, values)
-    outcome = patches.astype(F32) + jnp.dot(mixed, output_b, preferred_element_type=F32)
-    centred = outcome - jnp.mean(outcome, axis=-1, keepdims=True)
-    inverse = lax.rsqrt(jnp.mean(centred * centred, axis=-1, keepdims=True) + 1e-06)
-    normal_out = centred * inverse
-    signal = upstream.astype(F32)
-    d_outcome = inverse * (
-        signal
-        - jnp.mean(signal, axis=-1, keepdims=True)
-        - normal_out * jnp.mean(signal * normal_out, axis=-1, keepdims=True)
-    )
-    d_outcome = d_outcome.astype(BF)
-    grad_output = contract_rows(mixed, d_outcome)
-    d_mixed = lax.dot_general(
-        d_outcome, output_b, (((1,), (1,)), ((), ())), preferred_element_type=F32
-    ).astype(BF)
-    d_values = apply_back(attention, d_mixed)
-    grad_value = contract_rows(normed, d_values)
-    return grad_value.astype(BF), grad_output.astype(BF)
-
-
-def fold_output(rows, lead):
-    half = rows.reshape(lead + (56, 2, HID))
-    return jnp.swapaxes(half, -3, -2).reshape(lead + (BLOCKS, 16, HID))
-
-
-def unfold_output(blocks):
-    folded = blocks.reshape(-1, 2, 56, HID)
-    return jnp.swapaxes(folded, 1, 2).reshape(-1, D)
-
-
-def pack(grad_value, grad_output):
-    value = grad_value.reshape(2, 4, 2, BLOCKS, 16, HID)
-    output = fold_output(grad_output, (2, 4, 2))
-    both = jnp.concatenate([value, output], axis=0)
-    return both[..., :WIDTHS[0]], both[..., WIDTHS[0]:]
-
-
-def unpack(fulls):
-    both = jnp.concatenate(fulls, axis=-1)
-    return both[:2].reshape(D, HID), unfold_output(both[2:])
+        scratch_shapes=(
+            [pltpu.VMEM((4, 4, 2, BLOCKS, 16, w), BF) for w in WIDTHS]
+            + [pltpu.VMEM((4, 4, 2, BLOCKS, 16, w), BF) for w in WIDTHS]
+            + [pltpu.VMEM((2, BLOCKS, 16, w), BF) for w in WIDTHS]
+            + [
+                pltpu.VMEM((rows, D), BF),
+                pltpu.VMEM((112, 16, rows), BF),
+                pltpu.VMEM((HEADS, SEQ, SEQ), BF),
+                pltpu.VMEM((HEADS, SEQ, SEQ), BF),
+                pltpu.VMEM((rows, HID), F32),
+                pltpu.VMEM((rows, HID), BF),
+                pltpu.VMEM((56, 16, D), BF),
+                pltpu.VMEM((rows, HID), BF),
+                pltpu.VMEM((112, 8, rows), F32),
+                pltpu.VMEM((rows, D), F32),
+                pltpu.VMEM((rows, D), BF),
+                pltpu.VMEM((rows, HID), BF),
+            ]
+            + gather_scratch() + gather_scratch()
+            + [pltpu.VMEM((16, w), BF) for w in WIDTHS]
+            + line_sems() + line_sems() + line_sems(8)
+            + reduce_scratch()
+        ),
+        name="gradients",
+        compiler_params=pltpu.CompilerParams(
+            collective_id=0, has_side_effects=True, vmem_limit_bytes=60 * 2**20
+        ),
+    )(patches, queries, keys, upstream, own)
+
+
+def fold_output(rows):
+    half = rows.reshape(56, 2, HID)
+    return jnp.swapaxes(half, 0, 1).reshape(BLOCKS, 16, HID)
 
 
 def adam_update(weight, first, second, gradient):
@@ -575,25 +665,14 @@
 ):
     own = jnp.stack([
         value_weight.astype(BF).reshape(BLOCKS, 16, HID),
-        fold_output(output_weight.astype(BF), ()),
+        fold_output(output_weight.astype(BF)),
     ])
-    value_full, output_full = unpack(gather_weights(own))
-    normed = norm_rows(patches).astype(BF)
-    attention = attention_weights(queries, keys)
-    base = jnp.dot(normed, value_full, preferred_element_type=F32)
-    grads = local_grads(normed, patches, attention, upstream, base.astype(BF), output_full)
-    value_sum, output_sum = unpack(sum_and_gather(pack(*grads)))
-    squares = jnp.sum(value_sum.astype(F32) ** 2) + jnp.sum(output_sum.astype(F32) ** 2)
-    stretch = rho_scale / jnp.sqrt(squares / (2.0 * D * HID) + 1e-06)
-    values = base + stretch * jnp.dot(normed, value_sum, preferred_element_type=F32)
-    output_shifted = (output_full.astype(F32) + stretch * output_sum.astype(F32)).astype(BF)
-    grads = local_grads(normed, patches, attention, upstream, values.astype(BF), output_shifted)
-    owned = jnp.concatenate(sum_owned(pack(*grads)), axis=-1).astype(F32)
+    value_grad, output_grad = gradients(patches, queries, keys, upstream, own)
     value_new, value_first_new, value_second_new = adam_update(
-        value_weight, value_first, value_second, owned[0].reshape(112, HID)
+        value_weight, value_first, value_second, value_grad.reshape(112, HID).astype(F32)
     )
     output_new, output_first_new, output_second_new = adam_update(
-        output_weight, output_first, output_second, unfold_output(owned[1])
+        output_weight, output_first, output_second, output_grad
     )
     return (
         value_new,

time: 307 us -> 176 us (0.57)
  local copies, waits for them, and re-layouts: 63.3 us -> 0.06 us
  matrix products: 34 us -> 0 us
  other arithmetic: 36 us -> 5.43 us
    dot_general x14 -> x0, matrix products: 31.8 us -> none  [the longest x4 10.7 us: contract_rows(): lax.dot_general(left, right, (((0,), (0,)), ((), ())), preferred_element_...]
    reshape x6 -> x1, local copies, waits for them, and re-layouts: 23.8 us -> 0.02 us  [fold_output(): half = rows.reshape(56, 2, HID)]
    unnamed x58 -> x14, local copies, waits for them, and re-layouts: 18.6 us -> 0.04 us
    convert_element_type x3 -> x0, other arithmetic: 11.6 us -> none  [the longest x1 8.72 us: on_device(): (output_full.astype(F32) + stretch * output_sum.astype(F32)).astype(BF)]
    mul x1 -> x0, local copies, waits for them, and re-layouts: 8.81 us -> none  [on_device(): stretch * output_sum.astype(F32)]
    concatenate x4 -> x0, other arithmetic: 7.72 us -> none  [pack(): both = jnp.concatenate([value, output], axis=0)]
    reduce_sum x7 -> x0, other arithmetic: 7.31 us -> none  [the longest x1 2.62 us: on_device(): jnp.sum(output_sum.astype(F32) ** 2)]
    slice x3 -> x0, local copies, waits for them, and re-layouts: 6.27 us -> none  [the longest x2 6.21 us: unpack(): return (both[:2].reshape(D, HID), unfold_output(both[2:]))]
where the time goes in v2:
time: 176 us; the launch traced here: 173 us
  Pallas kernels  167 us (95%)
  other arithmetic  5.43 us (3%)
    pallas_call x1, Pallas kernels, gradients(): pl.pallas_call(kernel, out_shape=(jax.ShapeDtypeStruct((BLOCKS, 16, HID),...  167 us
    sub x2, other arithmetic, adam_update(): return (weight - learn_rate * update, first_new, second_new)  3.54 us

profile of v2, /device:TPU:8, one launch (start us, length us, event | category | flops | bytes accessed | tf_op | source)
XLA Modules:
  0.0 173.2 jit_solution(4193590281579338953)
XLA Ops:
  0.6 0.0 copy-start
  0.6 1.1 convert_element_type.13
  1.7 0.0 copy-done
  1.8 0.8 pad_maximum_fusion.own
  2.6 0.0 copy-start.1
  2.6 0.0 copy-start.4
  2.6 0.0 copy-start.5
  2.6 167.0 %gradients.1 = (bf16[7,16,896]{2,1,0:T(8,128)(2,1)}, f32[56,1792]{1,0:T(8,128)}) custom-call(bf16[256,1792]{1,0:T(8,128)(2,1)} %patches.1, bf16[256,896]{1,0:T(8,128)(2,1)} %queries.1, bf16[256,896]{1,0:T(8,128)(2,1)} %keys.1, bf16[256,1792]{1,0:T(8,128)(2,1)} %upstream.1, bf16[2,7,16,896]{3,2,1,0:T(8,128)(2,1)} %pad_maximum_fusion.own), custom_call_target="tpu_custom_call" | custom-call | tf_op jit(solution)/shard_map/gradients/pallas_call | solution.py:601
  169.6 0.0 copy-done.1
  169.6 0.0 copy-done.4
  169.6 0.0 copy-done.5
  169.6 0.0 copy-start.2
  169.6 0.0 copy-start.3
  169.7 0.0 copy-start.6
  169.7 2.3 %multiply_subtract_fusion = (f32[56,1792]{1,0:T(8,128)}, f32[56,1792]{1,0:T(8,128)}, f32[56,1792]{1,0:T(8,128)}) fusion(f32[56,1792]{1,0:T(8,128)S(1)} %copy-done.1, f32[56,1792]{1,0:T(8,128)} %get-tuple-element.9, f32[56,1792]{1,0:T(8,128)S(1)} %copy-done.4, f32[56,1792]{1,0:T(8,128)S(1)} %copy-done.5), kind=kLoop, calls=%fused_computation.8 | loop fusion | flops 1505280 | bytes 2809856 | tf_op jit(solution)/shard_map/sub | solution.py:651
  172.0 0.0 copy-done.2
  172.0 0.0 copy-done.3
  172.0 0.0 copy-done.6
  172.0 1.2 multiply_subtract_fusion.1
  (2 shorter events, 0.0 us)
Async XLA Ops:
  0.6 1.1 copy-start
  2.6 167.0 %copy-start.1 = (f32[56,1792]{1,0:T(8,128)S(1)}, f32[56,1792]{1,0:T(8,128)}, u32[]{:S(2)}) copy-start(f32[56,1792]{1,0:T(8,128)} %param.15) | copy-start | bytes 1204228
  2.6 167.0 %copy-start.4 = (f32[56,1792]{1,0:T(8,128)S(1)}, f32[56,1792]{1,0:T(8,128)}, u32[]{:S(2)}) copy-start(f32[56,1792]{1,0:T(8,128)} %param.17) | copy-start | bytes 1204228
  2.6 167.0 %copy-start.5 = (f32[56,1792]{1,0:T(8,128)S(1)}, f32[56,1792]{1,0:T(8,128)}, u32[]{:S(2)}) copy-start(f32[56,1792]{1,0:T(8,128)} %param.19) | copy-start | bytes 1204228
  169.6 2.3 %copy-start.2 = (f32[112,896]{1,0:T(8,128)S(1)}, f32[112,896]{1,0:T(8,128)}, u32[]{:S(2)}) copy-start(f32[112,896]{1,0:T(8,128)} %param.16) | copy-start | bytes 1204228
  169.6 2.3 %copy-start.3 = (f32[112,896]{1,0:T(8,128)S(1)}, f32[112,896]{1,0:T(8,128)}, u32[]{:S(2)}) copy-start(f32[112,896]{1,0:T(8,128)} %param.18) | copy-start | bytes 1204228
  169.7 2.3 %copy-start.6 = (bf16[7,16,896]{2,1,0:T(8,128)(2,1)S(1)}, bf16[7,16,896]{2,1,0:T(8,128)(2,1)}, u32[]{:S(2)}) copy-start(bf16[7,16,896]{2,1,0:T(8,128)(2,1)} %get-tuple-element.8) | copy-start | bytes 602116

commit v3 on v2

--- a/solution.py
+++ b/solution.py
@@ -11,7 +11,8 @@
 D = 1792
 HID = 896
 BLOCKS = 7
-WIDTHS = (512, 384)
+WIDTHS = (384, 384, 128)
+PARTS = (0, 1, 2)
 MESH = pl.DeviceIdType.MESH
 BF = jnp.bfloat16
 F32 = jnp.float32
@@ -55,6 +56,9 @@
             return device(self.x, (self.y + step) % 4, self.z, self.c)
         return device(self.x, self.y, (self.z + step) % 8, self.c)
 
+    def across(self, i, j):
+        return device((self.x + i) % 4, (self.y + j) % 4, self.z, self.c)
+
     def spot(self, axis, step=0):
         if axis == "x":
             return slot((self.x + step) % 4)
@@ -68,6 +72,7 @@
         targets += [self.along("x", s) for s in (1, 2, 3)]
         targets += [self.along("y", s) for s in (1, 2, 3)]
         targets += [self.along("z", s) for s in range(1, 8)]
+        targets += [self.across(i, j) for i in (1, 2, 3) for j in (1, 2, 3)]
         for t in targets:
             pl.semaphore_signal(sem, inc=1, device_id=t, device_id_type=MESH)
         pl.semaphore_wait(sem, len(targets))
@@ -102,7 +107,7 @@
 
 def reduce_scratch():
     shapes = []
-    for w in WIDTHS:
+    for w in WIDTHS[:2]:
         shapes += [
             pltpu.VMEM((4, 4, BLOCKS, 16, w), BF),
             pltpu.VMEM((4, 4, BLOCKS, 16, w), BF),
@@ -114,11 +119,131 @@
             pltpu.VMEM((7, 16, w), BF),
             pltpu.SemaphoreType.DMA((2, 4 + 2 + 4 + 3 + 7)),
         ]
-    return shapes
+    w = WIDTHS[2]
+    return shapes + [
+        pltpu.VMEM((4, 4, BLOCKS, 16, w), BF),
+        pltpu.VMEM((4, 4, BLOCKS, 16, w), BF),
+        pltpu.VMEM((2, 2, 4, 16, w), BF),
+        pltpu.VMEM((2, 3, 4, 4, 16, w), BF),
+        pltpu.VMEM((4, 4, 16, w), BF),
+        pltpu.VMEM((15, 16, w), BF),
+        pltpu.SemaphoreType.DMA((2, 1 + 8 + 15)),
+    ]
+
+
+ACROSS = [(i, j) for i in range(4) for j in range(4) if (i, j) != (0, 0)]
+
+
+class LineFirst:
+    def __init__(self, net, grads, out, scratch):
+        self.net, self.grads, self.out = net, grads, out
+        self.other, self.sums, self.far, self.ring, self.plane, self.from_plane, self.sem = scratch
+
+    def exchange(self):
+        net = self.net
+        self.core = push(self.grads.at[:, :, 1 - net.c], self.other, self.sem.at[0, 0], self.sem.at[1, 0], net.core())
+
+    def add_cores(self):
+        net = self.net
+        self.core.wait_recv()
+        g, other, sums = self.grads, self.other, self.sums
+
+        def write(i, v):
+            sums[i // 4, i % 4] = v
+
+        add_blocks(16, write, lambda i: g[i // 4, i % 4, net.c], lambda i: other[i // 4, i % 4])
+
+    def copy(self, k, way, j):
+        j = jnp.minimum(j, 6)
+        if k == 0:
+            src, dst = self.sums.at[pl.ds(2 * way, 2), :, j], self.far.at[way]
+        else:
+            src, dst = self.sums.at[:, :, j], self.ring.at[way, k - 1]
+        at = 1 + 2 * k + way
+        return pltpu.make_async_remote_copy(
+            src_ref=src, dst_ref=dst, send_sem=self.sem.at[0, at], recv_sem=self.sem.at[1, at],
+            device_id=self.net.along("z", (1, 7)[way]), device_id_type=MESH,
+        )
+
+    def sent(self, k, way):
+        return (self.net.z + ((4 - k) if way == 0 else (4 + k))) % 8
+
+    def got(self, k, way):
+        return (self.net.z + ((3 - k) if way == 0 else (5 + k))) % 8
+
+    def send(self, k):
+        for way in (0, 1):
+            j = self.sent(k, way)
+
+            @pl.when(j != 7)
+            def _():
+                self.copy(k, way, j).start()
+
+    def receive(self, k):
+        for way in (0, 1):
+            j = self.got(k, way)
+            at = jnp.minimum(j, 6)
+
+            @pl.when(j != 7)
+            def _():
+                self.copy(k, way, j).wait_recv()
+                if k == 0:
+                    rows = slice(2 * way, 2 * way + 2)
+                    self.sums[rows, :, at] = (self.sums[rows, :, at].astype(F32) + self.far[way].astype(F32)).astype(BF)
+                elif k < 3:
+                    self.sums[:, :, at] = (self.sums[:, :, at].astype(F32) + self.ring[way, k - 1].astype(F32)).astype(BF)
+
+    def plane_copy(self, e):
+        i, j = ACROSS[e]
+        net = self.net
+        return pltpu.make_async_remote_copy(
+            src_ref=self.plane.at[net.spot("x", i), net.spot("y", j)], dst_ref=self.from_plane.at[e],
+            send_sem=self.sem.at[0, 9 + e], recv_sem=self.sem.at[1, 9 + e], device_id=net.across(i, j), device_id_type=MESH,
+        )
+
+    def cross(self):
+        net = self.net
+
+        @pl.when(net.z != 7)
+        def _():
+            self.plane[...] = (
+                self.sums[:, :, net.z].astype(F32) + self.ring[0, 2].astype(F32) + self.ring[1, 2].astype(F32)
+            ).astype(BF)
+            for e in range(15):
+                self.plane_copy(e).start()
+
+    def finish(self):
+        net = self.net
+
+        @pl.when(net.z != 7)
+        def _():
+            for e in range(15):
+                self.plane_copy(e).wait_recv()
+            total = self.plane[net.spot("x"), net.spot("y")].astype(F32)
+            for e in range(15):
+                total = total + self.from_plane[e].astype(F32)
+            self.out[...] = total.astype(BF)
+
+    def drain(self):
+        self.core.wait_send()
+        for k in range(4):
+            for way in (0, 1):
+                j = self.sent(k, way)
+
+                @pl.when(j != 7)
+                def _():
+                    self.copy(k, way, j).wait_send()
+
+        @pl.when(self.net.z != 7)
+        def _():
+            for e in range(15):
+                self.plane_copy(e).wait_send()
 
 
 def reduce_all(net, grads, outs, scratch, make):
     make(1 - net.c)
+    ring = LineFirst(net, grads[2], outs[2], scratch[18:])
+    ring.exchange()
     state = []
     for part in (0, 1):
         state.append(scratch[part * 9:part * 9 + 9])
@@ -135,6 +260,8 @@
                 src, dst = grads[part].at[:, i, 1 - net.c], other.at[:, i]
             cores[part].append(push(src, dst, sem.at[0, j], sem.at[1, j], net.core()))
     make(net.c)
+    ring.add_cores()
+    ring.send(0)
 
     def half_of(ref, part, i, h):
         return ref.at[i, pl.ds(2 * h, 2)] if part == 0 else ref.at[pl.ds(2 * h, 2), i]
@@ -163,6 +290,9 @@
                 near[part][2] = push(half_of(sums, part, i, 1), mine.at[0, pl.ds(2, 2)], sem.at[0, 6], sem.at[1, 6], right)
             if step == 3:
                 near[part][3] = push(half_of(sums, part, i, 0), mine.at[1, pl.ds(0, 2)], sem.at[0, 7], sem.at[1, 7], left)
+        if j < 2:
+            ring.receive(j)
+            ring.send(j + 1)
     for part in (0, 1):
         other, sums, far, mine, _, _, _, _, sem = state[part]
         first = ordered(part)[0]
@@ -188,6 +318,8 @@
                 sums[k + 2, l] = v
             add_blocks(2, write, lambda k: sums[k + 2, l], lambda k: far[1, k])
         near[part][5] = push(half_of(sums, part, l, 1), mine.at[1, pl.ds(2, 2)], sem.at[0, 9], sem.at[1, 9], left)
+    ring.receive(2)
+    ring.send(3)
     second_copies = [[], []]
     for part in (0, 1):
         other, sums, far, mine, row, from_row, _, _, sem = state[part]
@@ -206,6 +338,8 @@
             second_copies[part].append(
                 push(row.at[net.spot(second, d)], from_row.at[d - 1], sem.at[0, 9 + d], sem.at[1, 9 + d], net.along(second, d))
             )
+    ring.receive(3)
+    ring.cross()
     for part in (0, 1):
         other, sums, far, mine, row, from_row, line, from_line, sem = state[part]
         second = ordered(part)[1]
@@ -222,6 +356,7 @@
             @pl.when(z != 7)
             def _():
                 push(line.at[z], from_line.at[d - 1], sem.at[0, 12 + d], sem.at[1, 12 + d], net.along("z", d))
+    ring.finish()
     for part in (0, 1):
         other, sums, far, mine, row, from_row, line, from_line, sem = state[part]
 
@@ -238,6 +373,7 @@
             outs[part][...] = total.astype(BF)
 
     def drain():
+        ring.drain()
         for part in (0, 1):
             other, sums, far, mine, row, from_row, line, from_line, sem = state[part]
             for copy in cores[part] + near[part] + second_copies[part]:
@@ -253,10 +389,113 @@
 
 
 def gather_scratch():
-    return [pltpu.SemaphoreType.DMA((2, 3 + 6 + 8)) for _ in WIDTHS]
-
-
-def gather_all(net, fulls, sems, between=()):
+    return [pltpu.SemaphoreType.DMA((2, 3 + 6 + 8)) for _ in WIDTHS[:2]] + [pltpu.SemaphoreType.DMA((2, 15 + 8 + 9))]
+
+
+class LineLast:
+    def __init__(self, net, full, sem):
+        self.net, self.full, self.sem = net, full, sem
+
+    def own(self, e):
+        i, j = ACROSS[e]
+        net = self.net
+        block = self.full.at[net.spot("x"), net.spot("y"), net.c, jnp.minimum(net.z, 6)]
+        return pltpu.make_async_remote_copy(
+            src_ref=block, dst_ref=block, send_sem=self.sem.at[0, e], recv_sem=self.sem.at[1, e],
+            device_id=net.across(i, j), device_id_type=MESH,
+        )
+
+    def start(self):
+        @pl.when(self.net.z != 7)
+        def _():
+            for e in range(15):
+                self.own(e).start()
+
+    def block(self, j, k, way):
+        j = jnp.minimum(j, 6)
+        if k == 4:
+            return self.full.at[pl.ds(2 * way, 2), :, self.net.c, j]
+        return self.full.at[:, :, self.net.c, j]
+
+    def copy(self, k, way, j):
+        at = 15 + 2 * (k - 1) + way
+        block = self.block(j, k, way)
+        return pltpu.make_async_remote_copy(
+            src_ref=block, dst_ref=block, send_sem=self.sem.at[0, at], recv_sem=self.sem.at[1, at],
+            device_id=self.net.along("z", (1, 7)[way]), device_id_type=MESH,
+        )
+
+    def core(self, k, way, j):
+        at = 23 if k == 0 else 24 + 2 * (k - 1) + way
+        block = self.block(j, k, way)
+        return pltpu.make_async_remote_copy(
+            src_ref=block, dst_ref=block, send_sem=self.sem.at[0, at], recv_sem=self.sem.at[1, at],
+            device_id=self.net.core(), device_id_type=MESH,
+        )
+
+    def sent(self, k, way):
+        return (self.net.z + ((9 - k) if way == 0 else (k - 1))) % 8
+
+    def got(self, k, way):
+        return (self.net.z + ((8 - k) if way == 0 else k)) % 8
+
+    def send(self, k):
+        for way in (0, 1):
+            j = self.sent(k, way)
+
+            @pl.when(j != 7)
+            def _():
+                self.copy(k, way, j).start()
+
+    def first(self):
+        net = self.net
+
+        @pl.when(net.z != 7)
+        def _():
+            for e in range(15):
+                self.own(e).wait_recv()
+            self.core(0, 0, net.z).start()
+
+        self.send(1)
+
+    def step(self, k):
+        for way in (0, 1):
+            j = self.got(k, way)
+
+            @pl.when(j != 7)
+            def _():
+                self.copy(k, way, j).wait_recv()
+                self.core(k, way, j).start()
+
+        if k < 4:
+            self.send(k + 1)
+
+    def finish(self):
+        net = self.net
+
+        @pl.when(net.z != 7)
+        def _():
+            self.core(0, 0, net.z).wait()
+            for e in range(15):
+                self.own(e).wait_send()
+
+        for k in (1, 2, 3, 4):
+            for way in (0, 1):
+                j = self.got(k, way)
+
+                @pl.when(j != 7)
+                def _():
+                    self.core(k, way, j).wait()
+
+                i = self.sent(k, way)
+
+                @pl.when(i != 7)
+                def _():
+                    self.copy(k, way, i).wait_send()
+
+
+def gather_all(net, fulls, sems, ring, between=()):
+    between = list(between) + [lambda: None] * 4
     seconds = [[], []]
     for part in (0, 1):
         second = ordered(part)[1]
@@ -274,8 +513,8 @@
 
     copies = [[], []]
     cores = [[], []]
-    if between:
-        between[0]()
+    between[0]()
+    ring.first()
     for part in (0, 1):
         first = ordered(part)[0]
         for copy in seconds[part]:
@@ -286,8 +525,10 @@
         for j, (h, to) in enumerate(((0, right), (1, left), (1, right), (0, left))):
             copies[part].append(push(line(part, me, h), line(part, me, h), sem.at[0, 3 + j], sem.at[1, 3 + j], to))
         cores[part].append(push(whole(part, me), whole(part, me), sem.at[0, 9], sem.at[1, 9], net.core()))
-    if between:
-        between[1]()
+    between[1]()
+    ring.step(1)
+    between[2]()
+    ring.step(2)
     for part in (0, 1):
         first = ordered(part)[0]
         right, left = net.along(first, 1), net.along(first, 3)
@@ -299,11 +540,16 @@
         copies[part].append(push(line(part, r, 1), line(part, r, 1), sem.at[0, 8], sem.at[1, 8], left))
         cores[part].append(push(line(part, l, 0), line(part, l, 0), sem.at[0, 10], sem.at[1, 10], net.core()))
         cores[part].append(push(line(part, r, 1), line(part, r, 1), sem.at[0, 11], sem.at[1, 11], net.core()))
-    for part in (0, 1):
-        first = ordered(part)[0]
-        r, l, far = net.spot(first, 1), net.spot(first, 3), net.spot(first, 2)
-        sem = sems[part]
-        for k, i, h in ((2, l, 1), (3, r, 0), (4, far, 0), (5, far, 1)):
+    between[3]()
+    ring.step(3)
+    for k in (2, 3, 4, 5):
+        if k == 4:
+            ring.step(4)
+        for part in (0, 1):
+            first = ordered(part)[0]
+            r, l, far = net.spot(first, 1), net.spot(first, 3), net.spot(first, 2)
+            sem = sems[part]
+            i, h = ((l, 1), (r, 0), (far, 0), (far, 1))[k - 2]
             copies[part][k].wait_recv()
             cores[part].append(push(line(part, i, h), line(part, i, h), sem.at[0, 10 + k], sem.at[1, 10 + k], net.core()))
     for part in (0, 1):
@@ -311,6 +557,7 @@
             copy.wait_recv()
         for copy in seconds[part] + copies[part] + cores[part]:
             copy.wait_send()
+    ring.finish()
 
 
 def spread_line(net, fulls, outs, sems):
@@ -360,7 +607,7 @@
             recv_sem=pairs[part].at[1, d], device_id=partner, device_id_type=MESH,
         )
 
-    for part in (0, 1):
+    for part in PARTS:
         @pl.when(net.z != 7)
         def _():
             owned[part][half, net.z] = outs[part][...]
@@ -372,7 +619,7 @@
 
         @pl.when(z != 7)
         def _():
-            for part in (0, 1):
+            for part in PARTS:
                 line_copy(part, d, z).wait_recv()
                 pair_copy(part, d, z).start()
     for d in range(8):
@@ -380,9 +627,9 @@
 
         @pl.when(z != 7)
         def _():
-            for part in (0, 1):
+            for part in PARTS:
                 pair_copy(part, d, z).wait()
-    for part in (0, 1):
+    for part in PARTS:
         @pl.when(net.z != 7)
         def _():
             for d in range(1, 8):
@@ -397,7 +644,7 @@
     lax.fori_loop(0, count, step, 0)
 
 
-STARTS = (0, WIDTHS[0])
+STARTS = (0, WIDTHS[0], WIDTHS[0] + WIDTHS[1])
 
 
 def norm_patches(patches, normed, normed_t):
@@ -417,8 +664,8 @@
     loop(14, turn)
 
 
-def attend(queries, keys, attention, attention_t):
-    for h in range(HEADS):
+def attend(queries, keys, attention, attention_t, heads):
+    for h in heads:
         q = queries[:, h * HD:(h + 1) * HD]
         k = keys[:, h * HD:(h + 1) * HD]
         scores = lax.dot_general(q, k, (((1,), (1,)), ((), ())), preferred_element_type=F32) * HD ** (-0.5)
@@ -429,7 +676,7 @@
 
 
 def project(normed, fulls, write):
-    for part in (0, 1):
+    for part in PARTS:
         w, at = WIDTHS[part], STARTS[part]
         total = jnp.dot(normed[:, :HID], fulls[part][0].reshape(HID, w), preferred_element_type=F32)
         total = total + jnp.dot(normed[:, HID:], fulls[part][1].reshape(HID, w), preferred_element_type=F32)
@@ -446,7 +693,7 @@
 
 def set_output(fulls, output, stretch):
     def step(i):
-        for part in (0, 1):
+        for part in PARTS:
             w = WIDTHS[part]
             for half, rows in enumerate(unfold(fulls[part], i)):
                 at = (pl.ds(i * BLOCKS, BLOCKS), slice(None), slice(half * HID + STARTS[part], half * HID + STARTS[part] + w))
@@ -460,7 +707,7 @@
 def sum_squares(fulls):
     def step(i, totals):
         out = []
-        for part in (0, 1):
+        for part in PARTS:
             block = fulls[part][i // 4, i % 4].astype(F32)
             block = block.reshape(2 * BLOCKS, 16, WIDTHS[part])
             out.append(totals[part] + jnp.sum(block * block, axis=0))
@@ -468,7 +715,7 @@
 
     totals = lax.fori_loop(0, 16, step, tuple(jnp.zeros((16, w), F32) for w in WIDTHS))
     parts = [jnp.sum(jnp.sum(t, axis=0, keepdims=True), axis=1, keepdims=True) for t in totals]
-    return parts[0] + parts[1]
+    return parts[0] + parts[1] + parts[2]
 
 
 def backward(patches, upstream, attention, attention_t, output, values, mixed, mixed_t, outcome, d_outcome, d_values):
@@ -520,32 +767,45 @@
         left = jnp.concatenate(rows, axis=0).astype(BF)
         got = jnp.dot(left, d_outcome[...], preferred_element_type=F32).reshape(4, 56, D)
         got = jnp.concatenate([got[:, :, :HID], got[:, :, HID:]], axis=1).astype(BF).reshape(4, BLOCKS, 16, HID)
-        for part in (0, 1):
+        for part in PARTS:
             grads[part][2 + hi, :, core] = got[..., STARTS[part]:STARTS[part] + WIDTHS[part]]
     for hi in (0, 1):
         rows = [normed_t[pl.ds((hi * 8 + y * 2 + core) * BLOCKS, BLOCKS)] for y in range(4)]
         left = jnp.concatenate(rows, axis=0).reshape(448, SEQ)
         got = jnp.dot(left, d_values[...], preferred_element_type=F32).astype(BF).reshape(4, BLOCKS, 16, HID)
-        for part in (0, 1):
+        for part in PARTS:
             grads[part][hi, :, core] = got[..., STARTS[part]:STARTS[part] + WIDTHS[part]]
 
 
 def kernel(
     patches, queries, keys, upstream, own,
     value_grad, output_grad,
-    full_a, full_b, grad_a, grad_b, owned_a, owned_b,
+    full_a, full_b, full_c, grad_a, grad_b, grad_c, owned_a, owned_b, owned_c, out_a, out_b, out_c,
     normed, normed_t, attention, attention_t, base, values, output,
     mixed, mixed_t, outcome, d_outcome, d_values,
-    sem_a, sem_b, again_a, again_b, out_a, out_b, line_a, line_b, last_a, last_b, pair_a, pair_b, *scratch,
+    sem_a, sem_b, sem_c, line_a, line_b, _, last_a, last_b, last_c, pair_a, pair_b, pair_c, *scratch,
 ):
     net = Net()
     net.barrier()
-    fulls, grads, outs, owned = (full_a, full_b), (grad_a, grad_b), (out_a, out_b), (owned_a, owned_b)
+    fulls, grads, outs = (full_a, full_b, full_c), (grad_a, grad_b, grad_c), (out_a, out_b, out_c)
+    owned, sems = (owned_a, owned_b, owned_c), (sem_a, sem_b)
     for part in (0, 1):
         fulls[part][net.spot("x"), net.spot("y"), net.c] = own[net.x % 2, :, :, STARTS[part]:STARTS[part] + WIDTHS[part]]
+
+    @pl.when(net.z != 7)
+    def _():
+        full_c[net.spot("x"), net.spot("y"), net.c, net.z] = own[net.x % 2, net.z, :, STARTS[2]:]
+
+    ring = LineLast(net, full_c, sem_c)
+    ring.start()
     gather_all(
-        net, fulls, (sem_a, sem_b),
-        (lambda: norm_patches(patches, normed, normed_t), lambda: attend(queries, keys, attention, attention_t)),
+        net, fulls, sems, ring,
+        (
+            lambda: norm_patches(patches, normed, normed_t),
+            lambda: attend(queries, keys, attention, attention_t, range(3)),
+            lambda: attend(queries, keys, attention, attention_t, range(3, 6)),
+            lambda: attend(queries, keys, attention, attention_t, range(6, 8)),
+        ),
     )
     set_output(fulls, output, None)
 
@@ -563,9 +823,15 @@
 
     back()
     drain = reduce_all(net, grads, outs, scratch, make)
+
+    @pl.when(net.z != 7)
+    def _():
+        full_c[net.spot("x"), net.spot("y"), net.c, net.z] = out_c[...]
+
     spread_line(net, fulls, outs, (line_a, line_b))
+    ring.start()
     wait_line(net, fulls, (line_a, line_b), True)
-    gather_all(net, fulls, (again_a, again_b))
+    gather_all(net, fulls, sems, ring)
     wait_line(net, fulls, (line_a, line_b), False)
     drain()
     mean_square = sum_squares(fulls) / (2.0 * D * HID)
@@ -578,9 +844,9 @@
     project(normed, fulls, write_values)
     back()
     drain = reduce_all(net, grads, outs, scratch, make)
-    share_owned(net, outs, owned, (last_a, last_b), (pair_a, pair_b))
+    share_owned(net, outs, owned, (last_a, last_b, last_c), (pair_a, pair_b, pair_c))
     drain()
-    for part in (0, 1):
+    for part in PARTS:
         w, at = WIDTHS[part], STARTS[part]
         value_grad[:, :, at:at + w] = owned[part][0]
         rows = owned[part][1].astype(F32).reshape(112, w)
@@ -590,10 +856,6 @@
 
 def vmem(n):
     return [pl.BlockSpec(memory_space=pltpu.VMEM)] * n
-
-
-def line_sems(n=7):
-    return [pltpu.SemaphoreType.DMA((2, n)) for _ in WIDTHS]
 
 
 def gradients(patches, queries, keys, upstream, own):
@@ -610,6 +872,7 @@
             [pltpu.VMEM((4, 4, 2, BLOCKS, 16, w), BF) for w in WIDTHS]
             + [pltpu.VMEM((4, 4, 2, BLOCKS, 16, w), BF) for w in WIDTHS]
             + [pltpu.VMEM((2, BLOCKS, 16, w), BF) for w in WIDTHS]
+            + [pltpu.VMEM((16, w), BF) for w in WIDTHS]
             + [
                 pltpu.VMEM((rows, D), BF),
                 pltpu.VMEM((112, 16, rows), BF),
@@ -624,9 +887,10 @@
                 pltpu.VMEM((rows, D), BF),
                 pltpu.VMEM((rows, HID), BF),
             ]
-            + gather_scratch() + gather_scratch()
-            + [pltpu.VMEM((16, w), BF) for w in WIDTHS]
-            + line_sems() + line_sems() + line_sems(8)
+            + gather_scratch()
+            + [pltpu.SemaphoreType.DMA((2, 7)) for _ in WIDTHS]
+            + [pltpu.SemaphoreType.DMA((2, 7)) for _ in WIDTHS]
+            + [pltpu.SemaphoreType.DMA((2, 8)) for _ in WIDTHS]
             + reduce_scratch()
         ),
         name="gradients",

time: 176 us -> 162 us (0.920); the launches traced: 173 us -> 161 us
  Pallas kernels: 167 us -> 155 us
    pallas_call x1, Pallas kernels: 167 us -> 155 us  [gradients(): pl.pallas_call(kernel, out_shape=(jax.ShapeDtypeStruct((BLOCKS, 16, HID),...]
where the time goes in v3:
time: 162 us; the launch traced here: 161 us
  Pallas kernels  155 us (96%)
  other arithmetic  5.43 us (3%)
    pallas_call x1, Pallas kernels, gradients(): pl.pallas_call(kernel, out_shape=(jax.ShapeDtypeStruct((BLOCKS, 16, HID),...  155 us
    sub x2, other arithmetic, adam_update(): return (weight - learn_rate * update, first_new, second_new)  3.54 us

profile of v3, /device:TPU:8, one launch (start us, length us, event | category | flops | bytes accessed | tf_op | source)
XLA Modules:
  0.0 161.4 jit_solution(782555627379110314)
XLA Ops:
  0.6 0.0 copy-start
  0.6 1.1 convert_element_type.13
  1.7 0.0 copy-done
  1.8 0.8 pad_maximum_fusion.own
  2.6 0.0 copy-start.1
  2.6 0.0 copy-start.4
  2.6 0.0 copy-start.5
  2.6 155.2 %gradients.1 = (bf16[7,16,896]{2,1,0:T(8,128)(2,1)}, f32[56,1792]{1,0:T(8,128)}) custom-call(bf16[256,1792]{1,0:T(8,128)(2,1)} %patches.1, bf16[256,896]{1,0:T(8,128)(2,1)} %queries.1, bf16[256,896]{1,0:T(8,128)(2,1)} %keys.1, bf16[256,1792]{1,0:T(8,128)(2,1)} %upstream.1, bf16[2,7,16,896]{3,2,1,0:T(8,128)(2,1)} %pad_maximum_fusion.own), custom_call_target="tpu_custom_call" | custom-call | tf_op jit(solution)/shard_map/gradients/pallas_call | solution.py:863
  157.8 0.0 copy-done.1
  157.8 0.0 copy-done.4
  157.8 0.0 copy-done.5
  157.8 0.0 copy-start.2
  157.8 0.0 copy-start.3
  157.8 0.0 copy-start.6
  157.9 2.3 %multiply_subtract_fusion = (f32[56,1792]{1,0:T(8,128)}, f32[56,1792]{1,0:T(8,128)}, f32[56,1792]{1,0:T(8,128)}) fusion(f32[56,1792]{1,0:T(8,128)S(1)} %copy-done.1, f32[56,1792]{1,0:T(8,128)} %get-tuple-element.9, f32[56,1792]{1,0:T(8,128)S(1)} %copy-done.4, f32[56,1792]{1,0:T(8,128)S(1)} %copy-done.5), kind=kLoop, calls=%fused_computation.8 | loop fusion | flops 1505280 | bytes 2809856 | tf_op jit(solution)/shard_map/sub | solution.py:915
  160.2 0.0 copy-done.2
  160.2 0.0 copy-done.3
  160.2 0.0 copy-done.6
  160.2 1.2 multiply_subtract_fusion.1
  (2 shorter events, 0.0 us)
Async XLA Ops:
  0.6 1.1 copy-start
  2.6 155.2 %copy-start.1 = (f32[56,1792]{1,0:T(8,128)S(1)}, f32[56,1792]{1,0:T(8,128)}, u32[]{:S(2)}) copy-start(f32[56,1792]{1,0:T(8,128)} %param.15) | copy-start | bytes 1204228
  2.6 155.2 %copy-start.4 = (f32[56,1792]{1,0:T(8,128)S(1)}, f32[56,1792]{1,0:T(8,128)}, u32[]{:S(2)}) copy-start(f32[56,1792]{1,0:T(8,128)} %param.17) | copy-start | bytes 1204228
  2.6 155.2 %copy-start.5 = (f32[56,1792]{1,0:T(8,128)S(1)}, f32[56,1792]{1,0:T(8,128)}, u32[]{:S(2)}) copy-start(f32[56,1792]{1,0:T(8,128)} %param.19) | copy-start | bytes 1204228
  157.8 2.3 %copy-start.2 = (f32[112,896]{1,0:T(8,128)S(1)}, f32[112,896]{1,0:T(8,128)}, u32[]{:S(2)}) copy-start(f32[112,896]{1,0:T(8,128)} %param.16) | copy-start | bytes 1204228
  157.8 2.3 %copy-start.3 = (f32[112,896]{1,0:T(8,128)S(1)}, f32[112,896]{1,0:T(8,128)}, u32[]{:S(2)}) copy-start(f32[112,896]{1,0:T(8,128)} %param.18) | copy-start | bytes 1204228
  157.8 2.3 %copy-start.6 = (bf16[7,16,896]{2,1,0:T(8,128)(2,1)S(1)}, bf16[7,16,896]{2,1,0:T(8,128)(2,1)}, u32[]{:S(2)}) copy-start(bf16[7,16,896]{2,1,0:T(8,128)(2,1)} %get-tuple-element.8) | copy-start | bytes 602116

commit v4 on v3

--- a/solution.py
+++ b/solution.py
@@ -66,7 +66,7 @@
             return (self.y + step) % 4
         return (self.z + step) % 8
 
-    def barrier(self):
+    def greet(self):
         sem = pltpu.get_barrier_semaphore()
         targets = [self.core()]
         targets += [self.along("x", s) for s in (1, 2, 3)]
@@ -75,7 +75,10 @@
         targets += [self.across(i, j) for i in (1, 2, 3) for j in (1, 2, 3)]
         for t in targets:
             pl.semaphore_signal(sem, inc=1, device_id=t, device_id_type=MESH)
-        pl.semaphore_wait(sem, len(targets))
+        return len(targets)
+
+    def meet(self, count):
+        pl.semaphore_wait(pltpu.get_barrier_semaphore(), count)
 
 
 def push(src, dst, send, recv, target):
@@ -290,9 +293,9 @@
                 near[part][2] = push(half_of(sums, part, i, 1), mine.at[0, pl.ds(2, 2)], sem.at[0, 6], sem.at[1, 6], right)
             if step == 3:
                 near[part][3] = push(half_of(sums, part, i, 0), mine.at[1, pl.ds(0, 2)], sem.at[0, 7], sem.at[1, 7], left)
-        if j < 2:
-            ring.receive(j)
-            ring.send(j + 1)
+        if j == 1:
+            ring.receive(0)
+            ring.send(1)
     for part in (0, 1):
         other, sums, far, mine, _, _, _, _, sem = state[part]
         first = ordered(part)[0]
@@ -318,8 +321,9 @@
                 sums[k + 2, l] = v
             add_blocks(2, write, lambda k: sums[k + 2, l], lambda k: far[1, k])
         near[part][5] = push(half_of(sums, part, l, 1), mine.at[1, pl.ds(2, 2)], sem.at[0, 9], sem.at[1, 9], left)
-    ring.receive(2)
-    ring.send(3)
+    for k in (1, 2):
+        ring.receive(k)
+        ring.send(k + 1)
     second_copies = [[], []]
     for part in (0, 1):
         other, sums, far, mine, row, from_row, _, _, sem = state[part]
@@ -389,7 +393,7 @@
 
 
 def gather_scratch():
-    return [pltpu.SemaphoreType.DMA((2, 3 + 6 + 8)) for _ in WIDTHS[:2]] + [pltpu.SemaphoreType.DMA((2, 15 + 8 + 9))]
+    return [pltpu.SemaphoreType.DMA((2, 16)) for _ in WIDTHS[:2]] + [pltpu.SemaphoreType.DMA((2, 15 + 8 + 9))]
 
 
 class LineLast:
@@ -494,98 +498,124 @@
                     self.copy(k, way, i).wait_send()
 
 
-def gather_all(net, fulls, sems, ring, between=()):
+def second_copy(net, fulls, sems, part, d, source):
+    second = ordered(part)[1]
+    x, y = net.spot("x"), net.spot("y")
+    if source:
+        x = net.spot("x", 4 - d) if second == "x" else x
+        y = net.spot("y", 4 - d) if second == "y" else y
+    chunk = fulls[part].at[x, y, net.c]
+    return pltpu.make_async_remote_copy(
+        src_ref=chunk, dst_ref=chunk, send_sem=sems[part].at[0, d - 1], recv_sem=sems[part].at[1, d - 1],
+        device_id=net.along(second, d), device_id_type=MESH,
+    )
+
+
+def gather_all(net, fulls, sems, ring, between=(), started=False):
     between = list(between) + [lambda: None] * 4
-    seconds = [[], []]
-    for part in (0, 1):
-        second = ordered(part)[1]
-        own = fulls[part].at[net.spot("x"), net.spot("y"), net.c]
-        for d in (2, 1, 3):
-            seconds[part].append(push(own, own, sems[part].at[0, d - 1], sems[part].at[1, d - 1], net.along(second, d)))
-
-    def line(part, i, h):
-        ref = fulls[part]
-        return ref.at[i, pl.ds(2 * h, 2), net.c] if part == 0 else ref.at[pl.ds(2 * h, 2), i, net.c]
-
-    def whole(part, i):
-        ref = fulls[part]
-        return ref.at[i, :, net.c] if part == 0 else ref.at[:, i, net.c]
-
-    copies = [[], []]
-    cores = [[], []]
+
+    def piece(part, i, h):
+        at = slice(None) if h is None else pl.ds(2 * h, 2)
+        return fulls[part].at[i, at, net.c] if part == 0 else fulls[part].at[at, i, net.c]
+
+    def send(part, step, h, at, to):
+        block = piece(part, net.spot(ordered(part)[0], step), h)
+        return push(block, block, sems[part].at[0, at], sems[part].at[1, at], to)
+
+    def ends(part):
+        first = ordered(part)[0]
+        return net.along(first, 1), net.along(first, 3)
+
+    rights, lefts, cores = [[], []], [[], []], [[], []]
     between[0]()
-    ring.first()
-    for part in (0, 1):
-        first = ordered(part)[0]
-        for copy in seconds[part]:
-            copy.wait_recv()
-        right, left = net.along(first, 1), net.along(first, 3)
-        me = net.spot(first)
-        sem = sems[part]
-        for j, (h, to) in enumerate(((0, right), (1, left), (1, right), (0, left))):
-            copies[part].append(push(line(part, me, h), line(part, me, h), sem.at[0, 3 + j], sem.at[1, 3 + j], to))
-        cores[part].append(push(whole(part, me), whole(part, me), sem.at[0, 9], sem.at[1, 9], net.core()))
+    if not started:
+        ring.first()
+    for part in (0, 1):
+        right, left = ends(part)
+        for d in (1, 2, 3):
+            second_copy(net, fulls, sems, part, d, True).wait_recv()
+        rights[part].append(send(part, 0, 0, 3, right))
+        lefts[part].append(send(part, 0, 1, 4, left))
+        rights[part].append(send(part, 0, 1, 5, right))
+        lefts[part].append(send(part, 0, 0, 6, left))
+        cores[part].append(send(part, 0, None, 9, net.core()))
     between[1]()
     ring.step(1)
     between[2]()
+    for part in (0, 1):
+        right, left = ends(part)
+        rights[part][0].wait_recv()
+        rights[part].append(send(part, 3, 0, 7, right))
+        lefts[part][0].wait_recv()
+        lefts[part].append(send(part, 1, 1, 8, left))
+        cores[part].append(send(part, 3, 0, 10, net.core()))
+        cores[part].append(send(part, 1, 1, 11, net.core()))
     ring.step(2)
-    for part in (0, 1):
-        first = ordered(part)[0]
-        right, left = net.along(first, 1), net.along(first, 3)
-        r, l = net.spot(first, 1), net.spot(first, 3)
-        sem = sems[part]
-        copies[part][0].wait_recv()
-        copies[part].append(push(line(part, l, 0), line(part, l, 0), sem.at[0, 7], sem.at[1, 7], right))
-        copies[part][1].wait_recv()
-        copies[part].append(push(line(part, r, 1), line(part, r, 1), sem.at[0, 8], sem.at[1, 8], left))
-        cores[part].append(push(line(part, l, 0), line(part, l, 0), sem.at[0, 10], sem.at[1, 10], net.core()))
-        cores[part].append(push(line(part, r, 1), line(part, r, 1), sem.at[0, 11], sem.at[1, 11], net.core()))
     between[3]()
     ring.step(3)
-    for k in (2, 3, 4, 5):
-        if k == 4:
-            ring.step(4)
-        for part in (0, 1):
-            first = ordered(part)[0]
-            r, l, far = net.spot(first, 1), net.spot(first, 3), net.spot(first, 2)
-            sem = sems[part]
-            i, h = ((l, 1), (r, 0), (far, 0), (far, 1))[k - 2]
-            copies[part][k].wait_recv()
-            cores[part].append(push(line(part, i, h), line(part, i, h), sem.at[0, 10 + k], sem.at[1, 10 + k], net.core()))
+    for part in (0, 1):
+        rights[part][1].wait_recv()
+        cores[part].append(send(part, 3, 1, 12, net.core()))
+        lefts[part][1].wait_recv()
+        cores[part].append(send(part, 1, 0, 13, net.core()))
+    ring.step(4)
+    for part in (0, 1):
+        rights[part][2].wait_recv()
+        cores[part].append(send(part, 2, 0, 14, net.core()))
+        lefts[part][2].wait_recv()
+        cores[part].append(send(part, 2, 1, 15, net.core()))
     for part in (0, 1):
         for copy in cores[part]:
             copy.wait_recv()
-        for copy in seconds[part] + copies[part] + cores[part]:
+        for copy in rights[part] + lefts[part] + cores[part]:
             copy.wait_send()
+        for d in (1, 2, 3):
+            second_copy(net, fulls, sems, part, d, False).wait_send()
     ring.finish()
 
 
-def spread_line(net, fulls, outs, sems):
-    for part in (0, 1):
-        @pl.when(net.z != 7)
-        def _():
-            dst = fulls[part].at[net.spot("x"), net.spot("y"), net.c, net.z]
-            dst[...] = outs[part][...]
-            for d in (4, 3, 5, 2, 6, 1, 7):
-                push(dst, dst, sems[part].at[0, d - 1], sems[part].at[1, d - 1], net.along("z", d))
-
-
-def wait_line(net, fulls, sems, recv):
-    for part in (0, 1):
-        for d in range(1, 8):
-            z = net.z if not recv else (net.z + 8 - d) % 8
-            block = fulls[part].at[net.spot("x"), net.spot("y"), net.c, jnp.minimum(z, 6)]
-
-            @pl.when(z != 7)
-            def _():
-                copy = pltpu.make_async_remote_copy(
-                    src_ref=block, dst_ref=block, send_sem=sems[part].at[0, d - 1], recv_sem=sems[part].at[1, d - 1],
-                    device_id=net.along("z", d), device_id_type=MESH,
-                )
-                if recv:
-                    copy.wait_recv()
-                else:
-                    copy.wait_send()
+def line_copy(net, fulls, lines, part, d, z):
+    block = fulls[part].at[net.spot("x"), net.spot("y"), net.c, jnp.minimum(z, 6)]
+    return pltpu.make_async_remote_copy(
+        src_ref=block, dst_ref=block, send_sem=lines[part].at[0, d - 1], recv_sem=lines[part].at[1, d - 1],
+        device_id=net.along("z", d), device_id_type=MESH,
+    )
+
+
+def spread_line(net, fulls, outs, sems, lines, ring):
+    def onward(part, z):
+        block = fulls[part].at[net.spot("x"), net.spot("y"), net.c, jnp.minimum(z, 6)]
+        for d in (2, 1, 3):
+            push(block, block, sems[part].at[0, d - 1], sems[part].at[1, d - 1], net.along(ordered(part)[1], d))
+
+    @pl.when(net.z != 7)
+    def _():
+        for part in (0, 1):
+            fulls[part][net.spot("x"), net.spot("y"), net.c, net.z] = outs[part][...]
+        for d in (4, 3, 5, 2, 6, 1, 7):
+            for part in (0, 1):
+                line_copy(net, fulls, lines, part, d, net.z).start()
+        for part in (0, 1):
+            onward(part, net.z)
+
+    for d in (1, 7, 2, 6, 3, 5, 4):
+        z = (net.z + 8 - d) % 8
+        if d == 3:
+            ring.first()
+
+        @pl.when(z != 7)
+        def _():
+            for part in (0, 1):
+                line_copy(net, fulls, lines, part, d, z).wait_recv()
+                onward(part, z)
+
+
+def drain_line(net, fulls, lines):
+    @pl.when(net.z != 7)
+    def _():
+        for part in (0, 1):
+            for d in range(1, 8):
+                line_copy(net, fulls, lines, part, d, net.z).wait_send()
 
 
 def share_owned(net, outs, owned, sems, pairs):
@@ -645,6 +675,15 @@
 
 
 STARTS = (0, WIDTHS[0], WIDTHS[0] + WIDTHS[1])
+
+
+def mean_signal(upstream, signal_mean):
+    def step(i):
+        at = pl.ds(pl.multiple_of(i * 64, 64), 64)
+        mean = jnp.mean(upstream[at, :].astype(F32), axis=-1, keepdims=True)
+        signal_mean[at, :] = jnp.broadcast_to(mean, (64, 128))
+
+    loop(4, step)
 
 
 def norm_patches(patches, normed, normed_t):
@@ -718,7 +757,7 @@
     return parts[0] + parts[1] + parts[2]
 
 
-def backward(patches, upstream, attention, attention_t, output, values, mixed, mixed_t, outcome, d_outcome, d_values):
+def backward(patches, upstream, signal_mean, attention, attention_t, output, values, mixed, mixed_t, outcome, d_outcome, d_values):
     for h in range(HEADS):
         at = slice(h * HD, (h + 1) * HD)
         mixed[:, at] = jnp.dot(attention[h], values[:, at], preferred_element_type=F32).astype(BF)
@@ -729,29 +768,30 @@
 
     loop(7, turn)
 
-    def columns(n):
-        at = pl.ds(pl.multiple_of(n * 256, 256), 256)
-        outcome[:, at] = patches[:, at].astype(F32) + jnp.dot(
-            mixed[...], output[:, :, at].reshape(HID, 256), preferred_element_type=F32
-        )
-
-    loop(7, columns)
+    outcome[...] = patches[...].astype(F32) + jnp.dot(
+        mixed[...], output[...].reshape(HID, D), preferred_element_type=F32
+    )
 
     def rows(i):
-        at = pl.ds(pl.multiple_of(i * 32, 32), 32)
-        total = outcome[at, :]
-        centred = total - jnp.mean(total, axis=-1, keepdims=True)
-        inverse = lax.rsqrt(jnp.mean(centred * centred, axis=-1, keepdims=True) + 1e-06)
-        normal = centred * inverse
-        signal = upstream[at, :].astype(F32)
-        grad = inverse * (
-            signal
-            - jnp.mean(signal, axis=-1, keepdims=True)
-            - normal * jnp.mean(signal * normal, axis=-1, keepdims=True)
-        )
-        d_outcome[at, :] = grad.astype(BF)
-
-    loop(8, rows)
+        at = pl.ds(pl.multiple_of(i * 128, 128), 128)
+        tiles = [slice(j * 128, j * 128 + 128) for j in range(14)]
+        total = outcome[at, tiles[0]]
+        for tile in tiles[1:]:
+            total = total + outcome[at, tile]
+        mean = jnp.sum(total, axis=-1, keepdims=True) / D
+        squares, cross = jnp.zeros((128, 128), F32), jnp.zeros((128, 128), F32)
+        for tile in tiles:
+            centred = outcome[at, tile] - mean
+            squares = squares + centred * centred
+            cross = cross + centred * upstream[at, tile].astype(F32)
+        inverse = lax.rsqrt(jnp.sum(squares, axis=-1, keepdims=True) / D + 1e-06)
+        slope = inverse * inverse * (jnp.sum(cross, axis=-1, keepdims=True) / D)
+        level = signal_mean[at, 0:1]
+        for tile in tiles:
+            centred = outcome[at, tile] - mean
+            d_outcome[at, tile] = (inverse * (upstream[at, tile].astype(F32) - level - centred * slope)).astype(BF)
+
+    loop(2, rows)
     d_mixed = lax.dot_general(
         d_outcome[...], output[...].reshape(HID, D), (((1,), (1,)), ((), ())), preferred_element_type=F32
     ).astype(BF)
@@ -778,31 +818,62 @@
 
 
 def kernel(
-    patches, queries, keys, upstream, own,
+    patches_hbm, queries_hbm, keys_hbm, upstream_hbm, value_rows, output_rows,
     value_grad, output_grad,
+    patches, queries, keys, upstream, own, signal_mean, load_sem,
     full_a, full_b, full_c, grad_a, grad_b, grad_c, owned_a, owned_b, owned_c, out_a, out_b, out_c,
     normed, normed_t, attention, attention_t, base, values, output,
     mixed, mixed_t, outcome, d_outcome, d_values,
     sem_a, sem_b, sem_c, line_a, line_b, _, last_a, last_b, last_c, pair_a, pair_b, pair_c, *scratch,
 ):
     net = Net()
-    net.barrier()
+    greeted = net.greet()
+    loads = []
+    for i, pair in enumerate(((patches_hbm, patches), (queries_hbm, queries), (keys_hbm, keys), (upstream_hbm, upstream))):
+        load = pltpu.make_async_copy(*pair, load_sem.at[i])
+        load.start()
+        loads.append(load)
     fulls, grads, outs = (full_a, full_b, full_c), (grad_a, grad_b, grad_c), (out_a, out_b, out_c)
-    owned, sems = (owned_a, owned_b, owned_c), (sem_a, sem_b)
-    for part in (0, 1):
-        fulls[part][net.spot("x"), net.spot("y"), net.c] = own[net.x % 2, :, :, STARTS[part]:STARTS[part] + WIDTHS[part]]
+    owned, sems, lines = (owned_a, owned_b, owned_c), (sem_a, sem_b), (line_a, line_b)
+
+    @pl.when(net.x % 2 == 0)
+    def _():
+        own[...] = value_rows[...].astype(BF).reshape(BLOCKS, 16, HID)
+
+    @pl.when(net.x % 2 == 1)
+    def _():
+        rows = jnp.concatenate([output_rows[:, :HID], output_rows[:, HID:]], axis=0)
+        own[...] = rows.astype(BF).reshape(BLOCKS, 16, HID)
+
+    for part in (0, 1):
+        fulls[part][net.spot("x"), net.spot("y"), net.c] = own[:, :, STARTS[part]:STARTS[part] + WIDTHS[part]]
 
     @pl.when(net.z != 7)
     def _():
-        full_c[net.spot("x"), net.spot("y"), net.c, net.z] = own[net.x % 2, net.z, :, STARTS[2]:]
-
+        full_c[net.spot("x"), net.spot("y"), net.c, net.z] = own[net.z, :, STARTS[2]:]
+
+    net.meet(greeted)
+    for part in (0, 1):
+        for d in (2, 1, 3):
+            second_copy(net, fulls, sems, part, d, False).start()
     ring = LineLast(net, full_c, sem_c)
     ring.start()
+
+    def prepare():
+        loads[0].wait()
+        norm_patches(patches, normed, normed_t)
+
+    def first_heads():
+        for load in loads[1:]:
+            load.wait()
+        attend(queries, keys, attention, attention_t, range(3))
+        mean_signal(upstream, signal_mean)
+
     gather_all(
         net, fulls, sems, ring,
         (
-            lambda: norm_patches(patches, normed, normed_t),
-            lambda: attend(queries, keys, attention, attention_t, range(3)),
+            prepare,
+            first_heads,
             lambda: attend(queries, keys, attention, attention_t, range(3, 6)),
             lambda: attend(queries, keys, attention, attention_t, range(6, 8)),
         ),
@@ -816,7 +887,7 @@
     project(normed, fulls, write_base)
 
     def back():
-        backward(patches, upstream, attention, attention_t, output, values, mixed, mixed_t, outcome, d_outcome, d_values)
+        backward(patches, upstream, signal_mean, attention, attention_t, output, values, mixed, mixed_t, outcome, d_outcome, d_values)
 
     def make(core):
         write_grads(core, normed_t, mixed_t, d_outcome, d_values, grads)
@@ -828,11 +899,10 @@
     def _():
         full_c[net.spot("x"), net.spot("y"), net.c, net.z] = out_c[...]
 
-    spread_line(net, fulls, outs, (line_a, line_b))
     ring.start()
-    wait_line(net, fulls, (line_a, line_b), True)
-    gather_all(net, fulls, sems, ring)
-    wait_line(net, fulls, (line_a, line_b), False)
+    spread_line(net, fulls, outs, sems, lines, ring)
+    gather_all(net, fulls, sems, ring, started=True)
+    drain_line(net, fulls, lines)
     drain()
     mean_square = sum_squares(fulls) / (2.0 * D * HID)
     stretch = rho_scale / jnp.sqrt(mean_square + 1e-06)
@@ -858,7 +928,7 @@
     return [pl.BlockSpec(memory_space=pltpu.VMEM)] * n
 
 
-def gradients(patches, queries, keys, upstream, own):
+def gradients(patches, queries, keys, upstream, value_weight, output_weight):
     rows = patches.shape[0]
     return pl.pallas_call(
         kernel,
@@ -866,10 +936,12 @@
             jax.ShapeDtypeStruct((BLOCKS, 16, HID), BF),
             jax.ShapeDtypeStruct((56, D), F32),
         ),
-        in_specs=vmem(5),
+        in_specs=[pl.BlockSpec(memory_space=pl.ANY)] * 4 + vmem(2),
         out_specs=vmem(2),
         scratch_shapes=(
-            [pltpu.VMEM((4, 4, 2, BLOCKS, 16, w), BF) for w in WIDTHS]
+            [pltpu.VMEM((rows, w), BF) for w in (D, HID, HID, D)]
+            + [pltpu.VMEM((BLOCKS, 16, HID), BF), pltpu.VMEM((rows, 128), F32), pltpu.SemaphoreType.DMA((4,))]
+            + [pltpu.VMEM((4, 4, 2, BLOCKS, 16, w), BF) for w in WIDTHS]
             + [pltpu.VMEM((4, 4, 2, BLOCKS, 16, w), BF) for w in WIDTHS]
             + [pltpu.VMEM((2, BLOCKS, 16, w), BF) for w in WIDTHS]
             + [pltpu.VMEM((16, w), BF) for w in WIDTHS]
@@ -897,12 +969,7 @@
         compiler_params=pltpu.CompilerParams(
             collective_id=0, has_side_effects=True, vmem_limit_bytes=60 * 2**20
         ),
-    )(patches, queries, keys, upstream, own)
-
-
-def fold_output(rows):
-    half = rows.reshape(56, 2, HID)
-    return jnp.swapaxes(half, 0, 1).reshape(BLOCKS, 16, HID)
+    )(patches, queries, keys, upstream, value_weight, output_weight)
 
 
 def adam_update(weight, first, second, gradient):
@@ -927,11 +994,7 @@
     value_second,
     output_second,
 ):
-    own = jnp.stack([
-        value_weight.astype(BF).reshape(BLOCKS, 16, HID),
-        fold_output(output_weight.astype(BF)),
-    ])
-    value_grad, output_grad = gradients(patches, queries, keys, upstream, own)
+    value_grad, output_grad = gradients(patches, queries, keys, upstream, value_weight, output_weight)
     value_new, value_first_new, value_second_new = adam_update(
         value_weight, value_first, value_second, value_grad.reshape(112, HID).astype(F32)
     )

time: 162 us -> 155 us (0.957)
  Pallas kernels: 155 us -> 149 us
  other arithmetic: 5.43 us -> 3.53 us
    pallas_call x1, Pallas kernels: 155 us -> 149 us  [gradients(): pl.pallas_call(kernel, out_shape=(jax.ShapeDtypeStruct((BLOCKS, 16, HID),...]
where the time goes in v4:
time: 155 us; the launch traced here: 153 us
  Pallas kernels  149 us (96%)
  other arithmetic  3.53 us (2%)
    pallas_call x1, Pallas kernels, gradients(): pl.pallas_call(kernel, out_shape=(jax.ShapeDtypeStruct((BLOCKS, 16, HID),...  149 us
    sub x2, other arithmetic, adam_update(): return (weight - learn_rate * update, first_new, second_new)  3.53 us

profile of v4, /device:TPU:8, one launch (start us, length us, event | category | flops | bytes accessed | tf_op | source)
XLA Modules:
  0.0 153.5 jit_solution(15989266096599392582)
XLA Ops:
  0.6 0.0 copy-start.1
  0.6 0.0 copy-start.4
  0.7 0.0 copy-start.5
  0.7 149.2 %gradients.1 = (bf16[7,16,896]{2,1,0:T(8,128)(2,1)}, f32[56,1792]{1,0:T(8,128)}) custom-call(bf16[256,1792]{1,0:T(8,128)(2,1)} %patches_hbm.1, bf16[256,896]{1,0:T(8,128)(2,1)} %queries_hbm.1, bf16[256,896]{1,0:T(8,128)(2,1)} %keys_hbm.1, bf16[256,1792]{1,0:T(8,128)(2,1)} %upstream_hbm.1, f32[112,896]{1,0:T(8,128)} %value_rows.1, f32[56,1792]{1,0:T(8,128)} %output_rows.1), custom_call_target="tpu_custom_call" | custom-call | tf_op jit(solution)/shard_map/gradients/pallas_call | solution.py:933
  149.9 0.0 copy-done.1
  149.9 0.0 copy-done.4
  149.9 0.0 copy-done.5
  149.9 0.0 copy-start
  149.9 0.0 copy-start.2
  149.9 0.0 copy-start.3
  149.9 0.0 copy-start.6
  149.9 2.3 %multiply_subtract_fusion = (f32[56,1792]{1,0:T(8,128)}, f32[56,1792]{1,0:T(8,128)}, f32[56,1792]{1,0:T(8,128)}) fusion(f32[56,1792]{1,0:T(8,128)S(1)} %copy-done.1, f32[56,1792]{1,0:T(8,128)} %get-tuple-element.9, f32[56,1792]{1,0:T(8,128)S(1)} %copy-done.4, f32[56,1792]{1,0:T(8,128)S(1)} %copy-done.5), kind=kLoop, calls=%fused_computation.7 | loop fusion | flops 1505280 | bytes 2809856 | tf_op jit(solution)/shard_map/sub | solution.py:982
  152.2 0.0 copy-done
  152.2 0.0 copy-done.2
  152.2 0.0 copy-done.3
  152.3 0.0 copy-done.6
  152.3 1.2 multiply_subtract_fusion.1
Async XLA Ops:
  0.6 149.2 %copy-start.1 = (f32[56,1792]{1,0:T(8,128)S(1)}, f32[56,1792]{1,0:T(8,128)}, u32[]{:S(2)}) copy-start(f32[56,1792]{1,0:T(8,128)} %output_rows.1) | copy-start | bytes 1204228
  0.6 149.2 %copy-start.4 = (f32[56,1792]{1,0:T(8,128)S(1)}, f32[56,1792]{1,0:T(8,128)}, u32[]{:S(2)}) copy-start(f32[56,1792]{1,0:T(8,128)} %param.17) | copy-start | bytes 1204228
  0.7 149.2 %copy-start.5 = (f32[56,1792]{1,0:T(8,128)S(1)}, f32[56,1792]{1,0:T(8,128)}, u32[]{:S(2)}) copy-start(f32[56,1792]{1,0:T(8,128)} %param.19) | copy-start | bytes 1204228
  149.9 2.4 %copy-start = (f32[112,896]{1,0:T(8,128)S(1)}, f32[112,896]{1,0:T(8,128)}, u32[]{:S(2)}) copy-start(f32[112,896]{1,0:T(8,128)} %value_rows.1) | copy-start | bytes 1204228
  149.9 2.3 %copy-start.2 = (f32[112,896]{1,0:T(8,128)S(1)}, f32[112,896]{1,0:T(8,128)}, u32[]{:S(2)}) copy-start(f32[112,896]{1,0:T(8,128)} %param.16) | copy-start | bytes 1204228
  149.9 2.3 %copy-start.3 = (f32[112,896]{1,0:T(8,128)S(1)}, f32[112,896]{1,0:T(8,128)}, u32[]{:S(2)}) copy-start(f32[112,896]{1,0:T(8,128)} %param.18) | copy-start | bytes 1204228
  149.9 2.3 %copy-start.6 = (bf16[7,16,896]{2,1,0:T(8,128)(2,1)S(1)}, bf16[7,16,896]{2,1,0:T(8,128)(2,1)}, u32[]{:S(2)}) copy-start(bf16[7,16,896]{2,1,0:T(8,128)(2,1)} %get-tuple-element.8) | copy-start | bytes 602116

commit v5 on v4

--- a/solution.py
+++ b/solution.py
@@ -120,7 +120,7 @@
             pltpu.VMEM((3, BLOCKS, 16, w), BF),
             pltpu.VMEM((BLOCKS, 16, w), BF),
             pltpu.VMEM((7, 16, w), BF),
-            pltpu.SemaphoreType.DMA((2, 4 + 2 + 4 + 3 + 7)),
+            pltpu.SemaphoreType.DMA((2, 4 + 2 + 4 + 3 + 7 + 3)),
         ]
     w = WIDTHS[2]
     return shapes + [
@@ -246,7 +246,6 @@
 def reduce_all(net, grads, outs, scratch, make):
     make(1 - net.c)
     ring = LineFirst(net, grads[2], outs[2], scratch[18:])
-    ring.exchange()
     state = []
     for part in (0, 1):
         state.append(scratch[part * 9:part * 9 + 9])
@@ -262,9 +261,9 @@
             else:
                 src, dst = grads[part].at[:, i, 1 - net.c], other.at[:, i]
             cores[part].append(push(src, dst, sem.at[0, j], sem.at[1, j], net.core()))
+        if step == 2:
+            ring.exchange()
     make(net.c)
-    ring.add_cores()
-    ring.send(0)
 
     def half_of(ref, part, i, h):
         return ref.at[i, pl.ds(2 * h, 2)] if part == 0 else ref.at[pl.ds(2 * h, 2), i]
@@ -293,7 +292,10 @@
                 near[part][2] = push(half_of(sums, part, i, 1), mine.at[0, pl.ds(2, 2)], sem.at[0, 6], sem.at[1, 6], right)
             if step == 3:
                 near[part][3] = push(half_of(sums, part, i, 0), mine.at[1, pl.ds(0, 2)], sem.at[0, 7], sem.at[1, 7], left)
-        if j == 1:
+        if j == 0:
+            ring.add_cores()
+            ring.send(0)
+        if j == 2:
             ring.receive(0)
             ring.send(1)
     for part in (0, 1):
@@ -338,28 +340,33 @@
             add_blocks(4, write, lambda k: sums[me, k], lambda k: mine[0, k], lambda k: mine[1, k])
         else:
             add_blocks(4, write, lambda k: sums[k, me], lambda k: mine[0, k], lambda k: mine[1, k])
-        for d in (2, 1, 3):
-            second_copies[part].append(
-                push(row.at[net.spot(second, d)], from_row.at[d - 1], sem.at[0, 9 + d], sem.at[1, 9 + d], net.along(second, d))
-            )
+        for g, blocks in enumerate((pl.ds(0, 4), pl.ds(4, 3))):
+            for d in (2, 1, 3):
+                at = (9 if g == 0 else 19) + d
+                second_copies[part].append(
+                    push(row.at[net.spot(second, d), blocks], from_row.at[d - 1, blocks], sem.at[0, at], sem.at[1, at], net.along(second, d))
+                )
     ring.receive(3)
     ring.cross()
-    for part in (0, 1):
-        other, sums, far, mine, row, from_row, line, from_line, sem = state[part]
-        second = ordered(part)[1]
-        me = net.spot(second)
-        for copy in second_copies[part]:
-            copy.wait_recv()
-
-        def write(k, v):
-            line[k] = v
-        add_blocks(BLOCKS, write, lambda k: row[me, k], lambda k: from_row[0, k], lambda k: from_row[1, k], lambda k: from_row[2, k])
-        for d in (4, 3, 5, 2, 6, 1, 7):
-            z = net.spot("z", d)
-
-            @pl.when(z != 7)
-            def _():
-                push(line.at[z], from_line.at[d - 1], sem.at[0, 12 + d], sem.at[1, 12 + d], net.along("z", d))
+    for g, (start, count) in enumerate(((0, 4), (4, 3))):
+        for part in (0, 1):
+            other, sums, far, mine, row, from_row, line, from_line, sem = state[part]
+            me = net.spot(ordered(part)[1])
+            for copy in second_copies[part][3 * g:3 * g + 3]:
+                copy.wait_recv()
+
+            def write(k, v):
+                line[start + k] = v
+            add_blocks(
+                count, write, lambda k: row[me, start + k], lambda k: from_row[0, start + k],
+                lambda k: from_row[1, start + k], lambda k: from_row[2, start + k],
+            )
+            for d in (4, 3, 5, 2, 6, 1, 7):
+                z = net.spot("z", d)
+
+                @pl.when((z >= start) & (z < start + count))
+                def _():
+                    push(line.at[z], from_line.at[d - 1], sem.at[0, 12 + d], sem.at[1, 12 + d], net.along("z", d))
     ring.finish()
     for part in (0, 1):
         other, sums, far, mine, row, from_row, line, from_line, sem = state[part]
@@ -393,7 +400,7 @@
 
 
 def gather_scratch():
-    return [pltpu.SemaphoreType.DMA((2, 16)) for _ in WIDTHS[:2]] + [pltpu.SemaphoreType.DMA((2, 15 + 8 + 9))]
+    return [pltpu.SemaphoreType.DMA((2, 16)) for _ in WIDTHS[:2]] + [pltpu.SemaphoreType.DMA((2, 15 + 16 + 17))]
 
 
 class LineLast:
@@ -415,42 +422,34 @@
             for e in range(15):
                 self.own(e).start()
 
-    def block(self, j, k, way):
-        j = jnp.minimum(j, 6)
-        if k == 4:
-            return self.full.at[pl.ds(2 * way, 2), :, self.net.c, j]
-        return self.full.at[:, :, self.net.c, j]
-
-    def copy(self, k, way, j):
-        at = 15 + 2 * (k - 1) + way
-        block = self.block(j, k, way)
+    def block(self, j, h):
+        return self.full.at[pl.ds(2 * h, 2), :, self.net.c, jnp.minimum(j, 6)]
+
+    def copy(self, k, way, j, h):
+        at = 15 + 4 * (k - 1) + 2 * way + h
+        block = self.block(j, h)
         return pltpu.make_async_remote_copy(
             src_ref=block, dst_ref=block, send_sem=self.sem.at[0, at], recv_sem=self.sem.at[1, at],
             device_id=self.net.along("z", (1, 7)[way]), device_id_type=MESH,
         )
 
-    def core(self, k, way, j):
-        at = 23 if k == 0 else 24 + 2 * (k - 1) + way
-        block = self.block(j, k, way)
+    def core(self, k, way, j, h):
+        at = 31 if k == 0 else 32 + 4 * (k - 1) + 2 * way + h
+        block = self.full.at[:, :, self.net.c, jnp.minimum(j, 6)] if k == 0 else self.block(j, h)
         return pltpu.make_async_remote_copy(
             src_ref=block, dst_ref=block, send_sem=self.sem.at[0, at], recv_sem=self.sem.at[1, at],
             device_id=self.net.core(), device_id_type=MESH,
         )
 
+    def halves(self, k, way):
+        return (way,) if k == 4 else (way, 1 - way)
+
     def sent(self, k, way):
         return (self.net.z + ((9 - k) if way == 0 else (k - 1))) % 8
 
     def got(self, k, way):
         return (self.net.z + ((8 - k) if way == 0 else k)) % 8
 
-    def send(self, k):
-        for way in (0, 1):
-            j = self.sent(k, way)
-
-            @pl.when(j != 7)
-            def _():
-                self.copy(k, way, j).start()
-
     def first(self):
         net = self.net
 
@@ -458,44 +457,45 @@
         def _():
             for e in range(15):
                 self.own(e).wait_recv()
-            self.core(0, 0, net.z).start()
-
-        self.send(1)
+            for at in (0, 1):
+                for way in (0, 1):
+                    self.copy(1, way, net.z, self.halves(1, way)[at]).start()
+            self.core(0, 0, net.z, 0).start()
 
     def step(self, k):
-        for way in (0, 1):
-            j = self.got(k, way)
-
-            @pl.when(j != 7)
-            def _():
-                self.copy(k, way, j).wait_recv()
-                self.core(k, way, j).start()
-
-        if k < 4:
-            self.send(k + 1)
+        for at in range(len(self.halves(k, 0))):
+            for way in (0, 1):
+                h = self.halves(k, way)[at]
+                j = self.got(k, way)
+
+                @pl.when(j != 7)
+                def _():
+                    self.copy(k, way, j, h).wait_recv()
+                    if k < 4 and h in self.halves(k + 1, way):
+                        self.copy(k + 1, way, j, h).start()
+                    self.core(k, way, j, h).start()
 
     def finish(self):
         net = self.net
 
         @pl.when(net.z != 7)
         def _():
-            self.core(0, 0, net.z).wait()
+            self.core(0, 0, net.z, 0).wait()
             for e in range(15):
                 self.own(e).wait_send()
 
         for k in (1, 2, 3, 4):
             for way in (0, 1):
-                j = self.got(k, way)
-
-                @pl.when(j != 7)
-                def _():
-                    self.core(k, way, j).wait()
-
-                i = self.sent(k, way)
-
-                @pl.when(i != 7)
-                def _():
-                    self.copy(k, way, i).wait_send()
+                for h in self.halves(k, way):
+                    j, i = self.got(k, way), self.sent(k, way)
+
+                    @pl.when(j != 7)
+                    def _():
+                        self.core(k, way, j, h).wait()
+
+                    @pl.when(i != 7)
+                    def _():
+                        self.copy(k, way, i, h).wait_send()
 
 
 def second_copy(net, fulls, sems, part, d, source):
@@ -542,6 +542,8 @@
     between[1]()
     ring.step(1)
     between[2]()
+    if started:
+        ring.step(2)
     for part in (0, 1):
         right, left = ends(part)
         rights[part][0].wait_recv()
@@ -550,7 +552,8 @@
         lefts[part].append(send(part, 1, 1, 8, left))
         cores[part].append(send(part, 3, 0, 10, net.core()))
         cores[part].append(send(part, 1, 1, 11, net.core()))
-    ring.step(2)
+    if not started:
+        ring.step(2)
     between[3]()
     ring.step(3)
     for part in (0, 1):

time: 155 us -> 150 us (0.968)
  Pallas kernels: 149 us -> 144 us
    pallas_call x1, Pallas kernels: 149 us -> 144 us  [gradients(): pl.pallas_call(kernel, out_shape=(jax.ShapeDtypeStruct((BLOCKS, 16, HID),...]
where the time goes in v5:
time: 150 us; the launch traced here: 148 us
  Pallas kernels  144 us (96%)
  other arithmetic  3.53 us (2%)
    pallas_call x1, Pallas kernels, gradients(): pl.pallas_call(kernel, out_shape=(jax.ShapeDtypeStruct((BLOCKS, 16, HID),...  144 us
    sub x2, other arithmetic, adam_update(): return (weight - learn_rate * update, first_new, second_new)  3.53 us

profile of v5, /device:TPU:8, one launch (start us, length us, event | category | flops | bytes accessed | tf_op | source)
XLA Modules:
  0.0 147.9 jit_solution(10730089644507322437)
XLA Ops:
  0.6 0.0 copy-start.1
  0.6 0.0 copy-start.4
  0.7 0.0 copy-start.5
  0.7 143.6 %gradients.1 = (bf16[7,16,896]{2,1,0:T(8,128)(2,1)}, f32[56,1792]{1,0:T(8,128)}) custom-call(bf16[256,1792]{1,0:T(8,128)(2,1)} %patches_hbm.1, bf16[256,896]{1,0:T(8,128)(2,1)} %queries_hbm.1, bf16[256,896]{1,0:T(8,128)(2,1)} %keys_hbm.1, bf16[256,1792]{1,0:T(8,128)(2,1)} %upstream_hbm.1, f32[112,896]{1,0:T(8,128)} %value_rows.1, f32[56,1792]{1,0:T(8,128)} %output_rows.1), custom_call_target="tpu_custom_call" | custom-call | tf_op jit(solution)/shard_map/gradients/pallas_call | solution.py:936
  144.2 0.0 copy-done.1
  144.2 0.0 copy-done.4
  144.2 0.0 copy-done.5
  144.3 0.0 copy-start
  144.3 0.0 copy-start.2
  144.3 0.0 copy-start.3
  144.3 0.0 copy-start.6
  144.3 2.3 %multiply_subtract_fusion = (f32[56,1792]{1,0:T(8,128)}, f32[56,1792]{1,0:T(8,128)}, f32[56,1792]{1,0:T(8,128)}) fusion(f32[56,1792]{1,0:T(8,128)S(1)} %copy-done.1, f32[56,1792]{1,0:T(8,128)} %get-tuple-element.9, f32[56,1792]{1,0:T(8,128)S(1)} %copy-done.4, f32[56,1792]{1,0:T(8,128)S(1)} %copy-done.5), kind=kLoop, calls=%fused_computation.7 | loop fusion | flops 1505280 | bytes 2809856 | tf_op jit(solution)/shard_map/sub | solution.py:985
  146.6 0.0 copy-done
  146.6 0.0 copy-done.2
  146.6 0.0 copy-done.3
  146.6 0.0 copy-done.6
  146.6 1.2 multiply_subtract_fusion.1
Async XLA Ops:
  0.6 143.6 %copy-start.1 = (f32[56,1792]{1,0:T(8,128)S(1)}, f32[56,1792]{1,0:T(8,128)}, u32[]{:S(2)}) copy-start(f32[56,1792]{1,0:T(8,128)} %output_rows.1) | copy-start | bytes 1204228
  0.6 143.6 %copy-start.4 = (f32[56,1792]{1,0:T(8,128)S(1)}, f32[56,1792]{1,0:T(8,128)}, u32[]{:S(2)}) copy-start(f32[56,1792]{1,0:T(8,128)} %param.17) | copy-start | bytes 1204228
  0.7 143.6 %copy-start.5 = (f32[56,1792]{1,0:T(8,128)S(1)}, f32[56,1792]{1,0:T(8,128)}, u32[]{:S(2)}) copy-start(f32[56,1792]{1,0:T(8,128)} %param.19) | copy-start | bytes 1204228
  144.3 2.4 %copy-start = (f32[112,896]{1,0:T(8,128)S(1)}, f32[112,896]{1,0:T(8,128)}, u32[]{:S(2)}) copy-start(f32[112,896]{1,0:T(8,128)} %value_rows.1) | copy-start | bytes 1204228
  144.3 2.3 %copy-start.2 = (f32[112,896]{1,0:T(8,128)S(1)}, f32[112,896]{1,0:T(8,128)}, u32[]{:S(2)}) copy-start(f32[112,896]{1,0:T(8,128)} %param.16) | copy-start | bytes 1204228
  144.3 2.3 %copy-start.3 = (f32[112,896]{1,0:T(8,128)S(1)}, f32[112,896]{1,0:T(8,128)}, u32[]{:S(2)}) copy-start(f32[112,896]{1,0:T(8,128)} %param.18) | copy-start | bytes 1204228
  144.3 2.3 %copy-start.6 = (bf16[7,16,896]{2,1,0:T(8,128)(2,1)S(1)}, bf16[7,16,896]{2,1,0:T(8,128)(2,1)}, u32[]{:S(2)}) copy-start(bf16[7,16,896]{2,1,0:T(8,128)(2,1)} %get-tuple-element.8) | copy-start | bytes 602116

commit v6 on v5

--- a/solution.py
+++ b/solution.py
@@ -621,52 +621,43 @@
                 line_copy(net, fulls, lines, part, d, net.z).wait_send()
 
 
-def share_owned(net, outs, owned, sems, pairs):
+def share_owned(net, outs, owned, lines, pairs):
     half = net.x % 2
     partner = device(net.x + 1 - 2 * half, net.y, net.z, net.c)
 
-    def block(part, z):
-        return owned[part].at[half, jnp.minimum(z, 6)]
-
-    def line_copy(part, d, z):
+    def copy(sems, at, z, target):
+        block = owned.at[half, jnp.minimum(z, 6)]
         return pltpu.make_async_remote_copy(
-            src_ref=block(part, z), dst_ref=block(part, z), send_sem=sems[part].at[0, d - 1],
-            recv_sem=sems[part].at[1, d - 1], device_id=net.along("z", d), device_id_type=MESH,
+            src_ref=block, dst_ref=block, send_sem=sems.at[0, at], recv_sem=sems.at[1, at], device_id=target, device_id_type=MESH,
         )
 
-    def pair_copy(part, d, z):
-        return pltpu.make_async_remote_copy(
-            src_ref=block(part, z), dst_ref=block(part, z), send_sem=pairs[part].at[0, d],
-            recv_sem=pairs[part].at[1, d], device_id=partner, device_id_type=MESH,
-        )
-
-    for part in PARTS:
-        @pl.when(net.z != 7)
-        def _():
-            owned[part][half, net.z] = outs[part][...]
-            for d in (4, 3, 5, 2, 6, 1, 7):
-                line_copy(part, d, net.z).start()
-            pair_copy(part, 0, net.z).start()
+    @pl.when(net.z != 7)
+    def _():
+        for part in PARTS:
+            owned[half, net.z, :, STARTS[part]:STARTS[part] + WIDTHS[part]] = outs[part][...]
+        for d in (4, 3, 5, 2, 6, 1, 7):
+            copy(lines, d - 1, net.z, net.along("z", d)).start()
+        copy(pairs, 0, net.z, partner).start()
+
     for d in (1, 7, 2, 6, 3, 5, 4):
         z = (net.z + 8 - d) % 8
 
         @pl.when(z != 7)
         def _():
-            for part in PARTS:
-                line_copy(part, d, z).wait_recv()
-                pair_copy(part, d, z).start()
+            copy(lines, d - 1, z, net.along("z", d)).wait_recv()
+            copy(pairs, d, z, partner).start()
+
     for d in range(8):
         z = (net.z + 8 - d) % 8
 
         @pl.when(z != 7)
         def _():
-            for part in PARTS:
-                pair_copy(part, d, z).wait()
-    for part in PARTS:
-        @pl.when(net.z != 7)
-        def _():
-            for d in range(1, 8):
-                line_copy(part, d, net.z).wait_send()
+            copy(pairs, d, z, partner).wait()
+
+    @pl.when(net.z != 7)
+    def _():
+        for d in range(1, 8):
+            copy(lines, d - 1, net.z, net.along("z", d)).wait_send()
 
 
 def loop(count, body):
@@ -765,12 +756,7 @@
         at = slice(h * HD, (h + 1) * HD)
         mixed[:, at] = jnp.dot(attention[h], values[:, at], preferred_element_type=F32).astype(BF)
 
-    def turn(j):
-        block = mixed[:, pl.ds(pl.multiple_of(j * 128, 128), 128)].astype(F32)
-        mixed_t[pl.ds(j * 16, 16)] = block.T.reshape(16, 8, SEQ)
-
-    loop(7, turn)
-
+    mixed_t[...] = mixed[...].T.astype(F32).reshape(112, 8, SEQ)
     outcome[...] = patches[...].astype(F32) + jnp.dot(
         mixed[...], output[...].reshape(HID, D), preferred_element_type=F32
     )
@@ -824,10 +810,10 @@
     patches_hbm, queries_hbm, keys_hbm, upstream_hbm, value_rows, output_rows,
     value_grad, output_grad,
     patches, queries, keys, upstream, own, signal_mean, load_sem,
-    full_a, full_b, full_c, grad_a, grad_b, grad_c, owned_a, owned_b, owned_c, out_a, out_b, out_c,
+    full_a, full_b, full_c, grad_a, grad_b, grad_c, owned, out_a, out_b, out_c,
     normed, normed_t, attention, attention_t, base, values, output,
     mixed, mixed_t, outcome, d_outcome, d_values,
-    sem_a, sem_b, sem_c, line_a, line_b, _, last_a, last_b, last_c, pair_a, pair_b, pair_c, *scratch,
+    sem_a, sem_b, sem_c, line_a, line_b, last, pairs, *scratch,
 ):
     net = Net()
     greeted = net.greet()
@@ -837,7 +823,7 @@
         load.start()
         loads.append(load)
     fulls, grads, outs = (full_a, full_b, full_c), (grad_a, grad_b, grad_c), (out_a, out_b, out_c)
-    owned, sems, lines = (owned_a, owned_b, owned_c), (sem_a, sem_b), (line_a, line_b)
+    sems, lines = (sem_a, sem_b), (line_a, line_b)
 
     @pl.when(net.x % 2 == 0)
     def _():
@@ -917,14 +903,12 @@
     project(normed, fulls, write_values)
     back()
     drain = reduce_all(net, grads, outs, scratch, make)
-    share_owned(net, outs, owned, (last_a, last_b, last_c), (pair_a, pair_b, pair_c))
+    share_owned(net, outs, owned, last, pairs)
     drain()
-    for part in PARTS:
-        w, at = WIDTHS[part], STARTS[part]
-        value_grad[:, :, at:at + w] = owned[part][0]
-        rows = owned[part][1].astype(F32).reshape(112, w)
-        output_grad[:, at:at + w] = rows[:56]
-        output_grad[:, HID + at:HID + at + w] = rows[56:]
+    value_grad[...] = owned[0]
+    rows = owned[1].astype(F32).reshape(112, HID)
+    output_grad[:, :HID] = rows[:56]
+    output_grad[:, HID:] = rows[56:]
 
 
 def vmem(n):
@@ -946,7 +930,7 @@
             + [pltpu.VMEM((BLOCKS, 16, HID), BF), pltpu.VMEM((rows, 128), F32), pltpu.SemaphoreType.DMA((4,))]
             + [pltpu.VMEM((4, 4, 2, BLOCKS, 16, w), BF) for w in WIDTHS]
             + [pltpu.VMEM((4, 4, 2, BLOCKS, 16, w), BF) for w in WIDTHS]
-            + [pltpu.VMEM((2, BLOCKS, 16, w), BF) for w in WIDTHS]
+            + [pltpu.VMEM((2, BLOCKS, 16, HID), BF)]
             + [pltpu.VMEM((16, w), BF) for w in WIDTHS]
             + [
                 pltpu.VMEM((rows, D), BF),
@@ -963,9 +947,8 @@
                 pltpu.VMEM((rows, HID), BF),
             ]
             + gather_scratch()
-            + [pltpu.SemaphoreType.DMA((2, 7)) for _ in WIDTHS]
-            + [pltpu.SemaphoreType.DMA((2, 7)) for _ in WIDTHS]
-            + [pltpu.SemaphoreType.DMA((2, 8)) for _ in WIDTHS]
+            + [pltpu.SemaphoreType.DMA((2, 7))] * 3
+            + [pltpu.SemaphoreType.DMA((2, 8))]
             + reduce_scratch()
         ),
         name="gradients",

time: 150 us -> 147 us (0.980)
  Pallas kernels: 144 us -> 141 us
    pallas_call x1, Pallas kernels: 144 us -> 141 us  [gradients(): pl.pallas_call(kernel, out_shape=(jax.ShapeDtypeStruct((BLOCKS, 16, HID),...]
where the time goes in v6:
time: 147 us; the launch traced here: 146 us
  Pallas kernels  141 us (96%)
  other arithmetic  3.53 us (2%)
    pallas_call x1, Pallas kernels, gradients(): pl.pallas_call(kernel, out_shape=(jax.ShapeDtypeStruct((BLOCKS, 16, HID),...  141 us
    sub x2, other arithmetic, adam_update(): return (weight - learn_rate * update, first_new, second_new)  3.53 us

profile of v6, /device:TPU:8, one launch (start us, length us, event | category | flops | bytes accessed | tf_op | source)
XLA Modules:
  0.0 145.7 jit_solution(18181635966411574362)
XLA Ops:
  0.6 0.0 copy-start.1
  0.6 0.0 copy-start.4
  0.7 0.0 copy-start.5
  0.7 141.4 %gradients.1 = (bf16[7,16,896]{2,1,0:T(8,128)(2,1)}, f32[56,1792]{1,0:T(8,128)}) custom-call(bf16[256,1792]{1,0:T(8,128)(2,1)} %patches_hbm.1, bf16[256,896]{1,0:T(8,128)(2,1)} %queries_hbm.1, bf16[256,896]{1,0:T(8,128)(2,1)} %keys_hbm.1, bf16[256,1792]{1,0:T(8,128)(2,1)} %upstream_hbm.1, f32[112,896]{1,0:T(8,128)} %value_rows.1, f32[56,1792]{1,0:T(8,128)} %output_rows.1), custom_call_target="tpu_custom_call" | custom-call | tf_op jit(solution)/shard_map/gradients/pallas_call | solution.py:920
  142.1 0.0 copy-done.1
  142.1 0.0 copy-done.4
  142.1 0.0 copy-done.5
  142.1 0.0 copy-start
  142.1 0.0 copy-start.2
  142.1 0.0 copy-start.3
  142.1 0.0 copy-start.6
  142.1 2.3 %multiply_subtract_fusion = (f32[56,1792]{1,0:T(8,128)}, f32[56,1792]{1,0:T(8,128)}, f32[56,1792]{1,0:T(8,128)}) fusion(f32[56,1792]{1,0:T(8,128)S(1)} %copy-done.1, f32[56,1792]{1,0:T(8,128)} %get-tuple-element.9, f32[56,1792]{1,0:T(8,128)S(1)} %copy-done.4, f32[56,1792]{1,0:T(8,128)S(1)} %copy-done.5), kind=kLoop, calls=%fused_computation.7 | loop fusion | flops 1505280 | bytes 2809856 | tf_op jit(solution)/shard_map/sub | solution.py:968
  144.4 0.0 copy-done
  144.4 0.0 copy-done.2
  144.4 0.0 copy-done.3
  144.5 0.0 copy-done.6
  144.5 1.2 multiply_subtract_fusion.1
Async XLA Ops:
  0.6 141.4 %copy-start.1 = (f32[56,1792]{1,0:T(8,128)S(1)}, f32[56,1792]{1,0:T(8,128)}, u32[]{:S(2)}) copy-start(f32[56,1792]{1,0:T(8,128)} %output_rows.1) | copy-start | bytes 1204228
  0.6 141.4 %copy-start.4 = (f32[56,1792]{1,0:T(8,128)S(1)}, f32[56,1792]{1,0:T(8,128)}, u32[]{:S(2)}) copy-start(f32[56,1792]{1,0:T(8,128)} %param.17) | copy-start | bytes 1204228
  0.7 141.4 %copy-start.5 = (f32[56,1792]{1,0:T(8,128)S(1)}, f32[56,1792]{1,0:T(8,128)}, u32[]{:S(2)}) copy-start(f32[56,1792]{1,0:T(8,128)} %param.19) | copy-start | bytes 1204228
  142.1 2.4 %copy-start = (f32[112,896]{1,0:T(8,128)S(1)}, f32[112,896]{1,0:T(8,128)}, u32[]{:S(2)}) copy-start(f32[112,896]{1,0:T(8,128)} %value_rows.1) | copy-start | bytes 1204228
  142.1 2.3 %copy-start.2 = (f32[112,896]{1,0:T(8,128)S(1)}, f32[112,896]{1,0:T(8,128)}, u32[]{:S(2)}) copy-start(f32[112,896]{1,0:T(8,128)} %param.16) | copy-start | bytes 1204228
  142.1 2.3 %copy-start.3 = (f32[112,896]{1,0:T(8,128)S(1)}, f32[112,896]{1,0:T(8,128)}, u32[]{:S(2)}) copy-start(f32[112,896]{1,0:T(8,128)} %param.18) | copy-start | bytes 1204228
  142.1 2.3 %copy-start.6 = (bf16[7,16,896]{2,1,0:T(8,128)(2,1)S(1)}, bf16[7,16,896]{2,1,0:T(8,128)(2,1)}, u32[]{:S(2)}) copy-start(bf16[7,16,896]{2,1,0:T(8,128)(2,1)} %get-tuple-element.8) | copy-start | bytes 602116
